TPU v7x, 512 devices: a whole 4x4x16 slice. The times are simulated.
512 devices in a mesh: group: 4 (over x_lo, core), blk: 16 (over z), local: 8 (over x_hi, y).
Axes of the slice: x: 4 (x_hi: 2, x_lo: 2; x = x_hi * 2 + x_lo), y: 4, z: 16, core: 2. Of those that a mesh axis runs over, the one named last changes fastest.
Arguments:
- tokens: bfloat16 [12288, 2048], P(('group', 'blk'), 'local'), may hold values from -6 to 6
- d_out: bfloat16 [12288, 2048], P(('group', 'blk'), 'local'), may hold values from -6 to 6
- ids: int32 [12288, 2], P(('group', 'blk')), may hold values from 0 to 7, all different within a row; in each aligned block of 192 rows (0 to 191, 192 to 383, ...) at most 64 rows name the same one
- gates: float32 [12288, 2], P(('group', 'blk')), may hold values from 0.1 to 1
- w_gate: bfloat16 [8, 2048, 1024], P('group', 'blk', 'local'), may hold values from -0.125 to 0.125
- w_up: bfloat16 [8, 2048, 1024], P('group', 'blk', 'local'), may hold values from -0.125 to 0.125
- w_down: bfloat16 [8, 1024, 2048], P('group', 'local', 'blk'), may hold values from -0.1875 to 0.1875
Outputs:
- moe_out: bfloat16 [12288, 2048], P(('group', 'blk'), 'local')
- grad_tokens: bfloat16 [12288, 2048], P(('group', 'blk'), 'local')
- grad_gates: float32 [12288, 2], P(('group', 'blk'))
- grad_gate: float32 [8, 2048, 1024], P('group', 'blk', 'local')
- grad_up: float32 [8, 2048, 1024], P('group', 'blk', 'local')
- grad_down: float32 [8, 1024, 2048], P('group', 'local', 'blk')
Inputs may be any that keep to these rules, and one draw needn't show every extreme that they name: `ids`: each row names 2 different experts; among the 192 rows of one block an expert is named by at most 64 rows, a bound that some block reaches; every expert is named somewhere.
All inputs are finite; a program needn't handle non-finite values.
Results may differ from a plain program's by a relative error of at most 0.02.
Values may be sent and summed in bfloat16 or wider, within the bound.
A program may use at most 64 MiB of HBM per device.

v0:
```python
import jax
import jax.numpy as jnp
from jax import lax
from jax.sharding import PartitionSpec as P


def shifted(x, axis, by):
    devices = lax.axis_size(axis)
    return lax.ppermute(x, axis, [(i, (i + by) % devices) for i in range(devices)])


def slot_numbers(id_block, experts, capacity):
    flat = id_block.reshape(-1)
    onehot = (flat[:, None] == jnp.arange(experts, dtype=jnp.int32)[None, :]).astype(jnp.int32)
    before = jnp.cumsum(onehot, axis=0) - onehot
    return flat * capacity + jnp.sum(before * onehot, axis=1)


def place_rows(rows, slot_index, total):
    return jnp.zeros((total, rows.shape[1]), rows.dtype).at[slot_index].set(rows)


def rounded(value):
    return lax.optimization_barrier(value.astype(jnp.bfloat16)).astype(jnp.float32)


def body(tokens, d_out, ids, gates, w_gate, w_up, w_down):
    group_count = lax.axis_size("group")
    blk_count = lax.axis_size("blk")
    tok_count = ids.shape[0]
    top_count = ids.shape[1]
    group_experts = w_gate.shape[0]
    experts = group_experts * group_count
    capacity = 4 * tok_count * top_count // (3 * experts)
    block_width = w_gate.shape[1]
    slot_index = slot_numbers(ids, experts, capacity)
    features = tokens.shape[1]
    token_pairs = jnp.broadcast_to(tokens[:, None, :], (tok_count, top_count, features))
    token_pairs = token_pairs.reshape(tok_count * top_count, features)
    grad_pairs = (gates[:, :, None] * d_out[:, None, :].astype(jnp.float32)).astype(jnp.bfloat16)
    grad_pairs = grad_pairs.reshape(tok_count * top_count, features)
    buffer_shape = (group_count, group_experts, capacity, features)
    token_slots = place_rows(token_pairs, slot_index, experts * capacity).reshape(buffer_shape)
    grad_slots = place_rows(grad_pairs, slot_index, experts * capacity).reshape(buffer_shape)
    token_slots, grad_slots = (token_slots, grad_slots)
    token_recv, grad_recv = (
        lax.all_to_all(token_slots, "group", split_axis=0, concat_axis=0, tiled=True),
        lax.all_to_all(grad_slots, "group", split_axis=0, concat_axis=0, tiled=True),
    )
    token_rows, grad_rows = (
        lax.all_gather(token_recv, "local", axis=3, tiled=True),
        lax.all_gather(grad_recv, "local", axis=3, tiled=True),
    )
    gate_full, up_full, down_full = (
        lax.all_gather(w_gate, "blk", axis=1, tiled=True),
        lax.all_gather(w_up, "blk", axis=1, tiled=True),
        lax.all_gather(w_down, "blk", axis=2, tiled=True),
    )
    pre_gate = jnp.einsum(
        "gecd,edf->gecf", token_rows, gate_full, preferred_element_type=jnp.float32
    )
    pre_up = jnp.einsum("gecd,edf->gecf", token_rows, up_full, preferred_element_type=jnp.float32)
    squashed = jax.nn.sigmoid(pre_gate)
    hidden = (pre_gate * squashed * pre_up).astype(jnp.bfloat16)
    out_terms = jnp.einsum("gecf,efd->gecd", hidden, down_full, preferred_element_type=jnp.float32)
    expert_rows = lax.psum_scatter(
        out_terms.astype(jnp.bfloat16), "local", scatter_dimension=3, tiled=True
    )
    d_hidden = jnp.einsum(
        "gecd,efd->gecf", grad_rows, down_full, preferred_element_type=jnp.float32
    )
    d_gate = (d_hidden * pre_up * squashed * (1.0 + pre_gate * (1.0 - squashed))).astype(
        jnp.bfloat16
    )
    d_up = (d_hidden * pre_gate * squashed).astype(jnp.bfloat16)
    input_terms = jnp.einsum(
        "gecf,edf->gecd", d_gate, gate_full, preferred_element_type=jnp.float32
    )
    input_terms = input_terms + jnp.einsum(
        "gecf,edf->gecd", d_up, up_full, preferred_element_type=jnp.float32
    )
    input_rows = lax.psum_scatter(
        input_terms.astype(jnp.bfloat16), "local", scatter_dimension=3, tiled=True
    )
    back_out, back_input = (
        lax.all_to_all(expert_rows, "group", split_axis=0, concat_axis=0, tiled=True),
        lax.all_to_all(input_rows, "group", split_axis=0, concat_axis=0, tiled=True),
    )

    def block_terms(start, count):
        token_part = lax.dynamic_slice_in_dim(token_rows, start, count, 3)
        grad_part = lax.dynamic_slice_in_dim(grad_rows, start, count, 3)
        term_gate = jnp.einsum(
            "gecd,gecf->def", token_part, d_gate, preferred_element_type=jnp.float32
        )
        term_up = jnp.einsum("gecd,gecf->def", token_part, d_up, preferred_element_type=jnp.float32)
        term_down = jnp.einsum(
            "gecf,gecd->def", hidden, grad_part, preferred_element_type=jnp.float32
        )
        return jnp.stack([term_gate, term_up, term_down], axis=2)

    position = lax.axis_index("blk")
    first_block = (position + blk_count - 1) % blk_count
    first = rounded(block_terms(first_block * block_width, block_width))

    def advance(step, carry):
        moved = shifted(carry.astype(jnp.bfloat16), "blk", 1).astype(carry.dtype)
        target = (position + blk_count - 1 - step) % blk_count
        return moved + rounded(block_terms(target * block_width, block_width))

    totals = lax.fori_loop(1, blk_count, advance, first)
    grad_gate = jnp.transpose(totals[:, :, 0, :], (1, 0, 2))
    grad_up = jnp.transpose(totals[:, :, 1, :], (1, 0, 2))
    grad_down = jnp.transpose(totals[:, :, 2, :], (1, 2, 0))
    slice_features = back_out.shape[3]
    out_pairs = back_out.reshape(experts * capacity, slice_features)[slot_index]
    out_pairs = out_pairs.reshape(tok_count, top_count, slice_features)
    input_pairs = back_input.reshape(experts * capacity, slice_features)[slot_index]
    input_pairs = input_pairs.reshape(tok_count, top_count, slice_features)
    moe_out = jnp.sum(gates[:, :, None] * out_pairs.astype(jnp.float32), axis=1).astype(
        jnp.bfloat16
    )
    grad_tokens = jnp.sum(input_pairs.astype(jnp.float32), axis=1).astype(jnp.bfloat16)
    gate_terms = jnp.sum(
        d_out[:, None, :].astype(jnp.float32) * out_pairs.astype(jnp.float32), axis=2
    )
    grad_gates = lax.psum(gate_terms, "local")
    return (moe_out, grad_tokens, grad_gates, grad_gate, grad_up, grad_down)


def solution(mesh):
    in_specs = (
        P(("group", "blk"), "local"),
        P(("group", "blk"), "local"),
        P(("group", "blk"), None),
        P(("group", "blk"), None),
        P("group", "blk", "local"),
        P("group", "blk", "local"),
        P("group", "local", "blk"),
    )
    out_specs = (
        P(("group", "blk"), "local"),
        P(("group", "blk"), "local"),
        P(("group", "blk"), None),
        P("group", "blk", "local"),
        P("group", "blk", "local"),
        P("group", "local", "blk"),
    )
    return jax.shard_map(body, mesh=mesh, in_specs=in_specs, out_specs=out_specs, check_vma=False)
```

profile of v0, /device:TPU:6, one launch (start us, length us, event | category | flops | bytes accessed | tf_op | source)
XLA Modules:
  0.0 614.8 jit_solution(7745023215637965429)
XLA Ops:
  14.3 7.6 %all_to_all.20 = bf16[4,2,64,256]{3,2,1,0:T(8,128)(2,1)S(1)} all-to-all(bf16[4,2,64,256]{3,2,1,0:T(8,128)(2,1)S(1)} %bitcast.158), channel_id=1, replica_groups=mesh['group'=4,'blk'=16,'local'=8] {'group'}, dimensions={0} | all-to-all | bytes 524288 | tf_op jit(solution)/shard_map/all_to_all | solution.py:47
  27.2 8.4 %all_to_all.21 = bf16[4,2,64,256]{3,2,1,0:T(8,128)(2,1)S(1)} all-to-all(bf16[4,2,64,256]{3,2,1,0:T(8,128)(2,1)S(1)} %bitcast.157), channel_id=1, replica_groups=mesh['group'=4,'blk'=16,'local'=8] {'group'}, dimensions={0} | all-to-all | bytes 524288 | tf_op jit(solution)/shard_map/all_to_all | solution.py:48
  36.5 49.2 %all-gather.10.cloned.1.call-done = bf16[2,2048,128]{2,1,0:T(8,128)(2,1)} async-done(((bf16[2,128,128]{2,1,0:T(8,128)(2,1)}), bf16[2,2048,128]{2,1,0:T(8,128)(2,1)}) %all-gather.10.cloned.1.call-update) | async-done | bytes 1048592 | tf_op jit(solution)/shard_map/all_gather | solution.py:56
  85.6 68.1 %all-gather.6.cloned.1.call-done = bf16[4,2,64,2048]{3,2,0,1:T(8,128)(2,1)} async-done(((bf16[4,2,64,256]{3,2,0,1:T(8,128)(2,1)}), bf16[4,2,64,2048]{3,2,0,1:T(8,128)(2,1)}) %all-gather.6.cloned.1.call-update) | async-done | bytes 2097168 | tf_op jit(solution)/shard_map/all_gather | solution.py:51
  157.2 69.3 %all-gather.8.cloned.1.call-done = bf16[2,2048,128]{2,1,0:T(8,128)(2,1)} async-done(((bf16[2,128,128]{2,1,0:T(8,128)(2,1)}), bf16[2,2048,128]{2,1,0:T(8,128)(2,1)}) %all-gather.8.cloned.1.call-update) | async-done | bytes 1048592 | tf_op jit(solution)/shard_map/all_gather | solution.py:55
  229.2 68.5 %all-gather.12.cloned.1.call-done = bf16[2,128,2048]{2,1,0:T(8,128)(2,1)} async-done(((bf16[2,128,128]{2,1,0:T(8,128)(2,1)}), bf16[2,128,2048]{2,1,0:T(8,128)(2,1)}) %all-gather.12.cloned.1.call-update) | async-done | bytes 1048592 | tf_op jit(solution)/shard_map/all_gather | solution.py:57
  297.7 67.0 %all-gather.14.cloned.1.call-done = bf16[4,2,64,2048]{3,2,0,1:T(8,128)(2,1)} async-done(((bf16[4,2,64,256]{3,2,0,1:T(8,128)(2,1)}), bf16[4,2,64,2048]{3,2,0,1:T(8,128)(2,1)}) %all-gather.14.cloned.1.call-update) | async-done | bytes 2097168 | tf_op jit(solution)/shard_map/all_gather | solution.py:52
  376.2 139.1 %while.15 = (s32[]{:T(128)}, f32[128,2,3,128]{3,0,1,2:T(8,128)S(1)}, s32[]{:T(128)}, bf16[4,2,64,2048]{3,2,0,1:T(8,128)(2,1)S(1)}, bf16[4,2,64,128]{3,2,0,1:T(8,...) while((s32[]{:T(128)}, ...), condition=%wide.region_12.13_spmd, body=%wide.region_11.12_spmd.sunk | while | flops 51019792 | bytes 3539296 | solution.py:111
  381.5 5.3 collective-permute-done
  390.5 5.2 collective-permute-done
  408.2 5.2 collective-permute-done
  417.1 5.2 collective-permute-done
  425.9 5.2 collective-permute-done
  434.8 6.3 %collective-permute-done = bf16[128,2,3,128]{3,0,1,2:T(8,128)(2,1)S(1)} collective-permute-done((bf16[128,2,3,128]{3,0,1,2:T(8,128)(2,1)S(1)}, bf16[128,2,3,128]{3,0,1,2:T(8,128)(2,1)S(1)}, u32[]{:S(2)}, u32[]{:S(2)}) %collective-permute-start) | collective-permute-done | bytes 196640 | tf_op jit(solution)/shard_map/while/body/eval_jaxpr/ppermute | solution.py:9
  444.9 7.1 %collective-permute-done = bf16[128,2,3,128]{3,0,1,2:T(8,128)(2,1)S(1)} collective-permute-done((bf16[128,2,3,128]{3,0,1,2:T(8,128)(2,1)S(1)}, bf16[128,2,3,128]{3,0,1,2:T(8,128)(2,1)S(1)}, u32[]{:S(2)}, u32[]{:S(2)}) %collective-permute-start) | collective-permute-done | bytes 196640 | tf_op jit(solution)/shard_map/while/body/eval_jaxpr/ppermute | solution.py:9
  455.6 6.2 %collective-permute-done = bf16[128,2,3,128]{3,0,1,2:T(8,128)(2,1)S(1)} collective-permute-done((bf16[128,2,3,128]{3,0,1,2:T(8,128)(2,1)S(1)}, bf16[128,2,3,128]{3,0,1,2:T(8,128)(2,1)S(1)}, u32[]{:S(2)}, u32[]{:S(2)}) %collective-permute-start) | collective-permute-done | bytes 196640 | tf_op jit(solution)/shard_map/while/body/eval_jaxpr/ppermute | solution.py:9
  465.6 5.3 collective-permute-done
  474.6 5.2 collective-permute-done
  483.5 5.2 collective-permute-done
  492.4 5.2 collective-permute-done
  501.2 5.2 collective-permute-done
  510.1 5.2 collective-permute-done
  521.3 30.8 %reduce-scatter.5.cloned.1.call-done = bf16[4,2,64,256]{3,2,0,1:T(8,128)(2,1)} async-done(((bf16[4,2,64,2048]{3,2,0,1:T(8,128)(2,1)}), bf16[4,2,64,256]{3,2,0,1:T(8,128)(2,1)}) %reduce-scatter.5.cloned.1.call-update) | async-done | bytes 262160 | tf_op jit(solution)/shard_map/reduce_scatter | solution.py:82
  562.4 41.6 %psum.7 = f32[192,2]{1,0:T(8,128)S(1)} all-reduce(f32[192,2]{1,0:T(8,128)S(1)} %get-tuple-element.240), channel_id=1, replica_groups=mesh['group'=4,'blk'=16,'local'=8] {'local'}, use_global_device_ids=true, to_apply=%region_10.11 | all-reduce | flops 384 | bytes 3072 | tf_op jit(solution)/shard_map/psum | solution.py:127
  (188 shorter events, 111.9 us)
Async XLA Ops:
  7.2 78.5 %all-gather.10.cloned.1.call-start = ((), (), s32[]{:S(2)}) async-start(), calls=%async_computation.8 | async-start | bytes 1114112 | tf_op jit(solution)/shard_map/all_gather | solution.py:56
  7.9 145.9 %all-gather.6.cloned.1.call-start = ((), (), s32[]{:S(2)}) async-start(), calls=%async_computation.6 | async-start | bytes 2359296 | tf_op jit(solution)/shard_map/all_gather | solution.py:51
  22.7 203.8 %all-gather.8.cloned.1.call-start = ((), (), s32[]{:S(2)}) async-start(), calls=%async_computation.7 | async-start | bytes 1114112 | tf_op jit(solution)/shard_map/all_gather | solution.py:55
  23.4 274.3 %all-gather.12.cloned.1.call-start = ((), (), s32[]{:S(2)}) async-start(), calls=%async_computation.9 | async-start | bytes 1114112 | tf_op jit(solution)/shard_map/all_gather | solution.py:57
  24.0 340.7 %all-gather.14.cloned.1.call-start = ((), (), s32[]{:S(2)}) async-start(), calls=%async_computation.11 | async-start | bytes 2359296 | tf_op jit(solution)/shard_map/all_gather | solution.py:52
  36.4 479.1 %reduce-scatter.3.cloned.1.call-start = ((), (), s32[]{:S(2)}) async-start(), calls=%async_computation.10 | async-start | bytes 2359296 | tf_op jit(solution)/shard_map/reduce_scatter | solution.py:66
  369.4 182.7 %reduce-scatter.5.cloned.1.call-start = ((), (), s32[]{:S(2)}) async-start(), calls=%async_computation.12 | async-start | bytes 2359296 | tf_op jit(solution)/shard_map/reduce_scatter | solution.py:82
  376.3 10.4 %collective-permute-start = (bf16[128,2,3,128]{3,0,1,2:T(8,128)(2,1)S(1)}, bf16[128,2,3,128]{3,0,1,2:T(8,128)(2,1)S(1)}, u32[]{:S(2)}, u32[]{:S(2)}) collective-permute-start(bf16[128,2,3,128]{3,0,1,2:T(8,128)(2,1)S(1)} %convert_element_type.131), channel_id=1, source_target_pairs={{0,8},{8,16},{16,24},{24,32},{32,40},{40,48},{48,56},{56,64},{64,7... | collective-permute-start | bytes 589832 | tf_op jit(solution)/shard_map/while/body/eval_jaxpr/ppermute | solution.py:9
  386.8 8.8 %collective-permute-start = (bf16[128,2,3,128]{3,0,1,2:T(8,128)(2,1)S(1)}, bf16[128,2,3,128]{3,0,1,2:T(8,128)(2,1)S(1)}, u32[]{:S(2)}, u32[]{:S(2)}) collective-permute-start(bf16[128,2,3,128]{3,0,1,2:T(8,128)(2,1)S(1)} %convert_element_type.131), channel_id=1, source_target_pairs={{0,8},{8,16},{16,24},{24,32},{32,40},{40,48},{48,56},{56,64},{64,7... | collective-permute-start | bytes 589832 | tf_op jit(solution)/shard_map/while/body/eval_jaxpr/ppermute | solution.py:9
  395.7 8.8 %collective-permute-start = (bf16[128,2,3,128]{3,0,1,2:T(8,128)(2,1)S(1)}, bf16[128,2,3,128]{3,0,1,2:T(8,128)(2,1)S(1)}, u32[]{:S(2)}, u32[]{:S(2)}) collective-permute-start(bf16[128,2,3,128]{3,0,1,2:T(8,128)(2,1)S(1)} %convert_element_type.131), channel_id=1, source_target_pairs={{0,8},{8,16},{16,24},{24,32},{32,40},{40,48},{48,56},{56,64},{64,7... | collective-permute-start | bytes 589832 | tf_op jit(solution)/shard_map/while/body/eval_jaxpr/ppermute | solution.py:9
  404.6 8.8 %collective-permute-start = (bf16[128,2,3,128]{3,0,1,2:T(8,128)(2,1)S(1)}, bf16[128,2,3,128]{3,0,1,2:T(8,128)(2,1)S(1)}, u32[]{:S(2)}, u32[]{:S(2)}) collective-permute-start(bf16[128,2,3,128]{3,0,1,2:T(8,128)(2,1)S(1)} %convert_element_type.131), channel_id=1, source_target_pairs={{0,8},{8,16},{16,24},{24,32},{32,40},{40,48},{48,56},{56,64},{64,7... | collective-permute-start | bytes 589832 | tf_op jit(solution)/shard_map/while/body/eval_jaxpr/ppermute | solution.py:9
  413.5 8.8 %collective-permute-start = (bf16[128,2,3,128]{3,0,1,2:T(8,128)(2,1)S(1)}, bf16[128,2,3,128]{3,0,1,2:T(8,128)(2,1)S(1)}, u32[]{:S(2)}, u32[]{:S(2)}) collective-permute-start(bf16[128,2,3,128]{3,0,1,2:T(8,128)(2,1)S(1)} %convert_element_type.131), channel_id=1, source_target_pairs={{0,8},{8,16},{16,24},{24,32},{32,40},{40,48},{48,56},{56,64},{64,7... | collective-permute-start | bytes 589832 | tf_op jit(solution)/shard_map/while/body/eval_jaxpr/ppermute | solution.py:9
  422.3 8.8 %collective-permute-start = (bf16[128,2,3,128]{3,0,1,2:T(8,128)(2,1)S(1)}, bf16[128,2,3,128]{3,0,1,2:T(8,128)(2,1)S(1)}, u32[]{:S(2)}, u32[]{:S(2)}) collective-permute-start(bf16[128,2,3,128]{3,0,1,2:T(8,128)(2,1)S(1)} %convert_element_type.131), channel_id=1, source_target_pairs={{0,8},{8,16},{16,24},{24,32},{32,40},{40,48},{48,56},{56,64},{64,7... | collective-permute-start | bytes 589832 | tf_op jit(solution)/shard_map/while/body/eval_jaxpr/ppermute | solution.py:9
  431.2 9.9 %collective-permute-start = (bf16[128,2,3,128]{3,0,1,2:T(8,128)(2,1)S(1)}, bf16[128,2,3,128]{3,0,1,2:T(8,128)(2,1)S(1)}, u32[]{:S(2)}, u32[]{:S(2)}) collective-permute-start(bf16[128,2,3,128]{3,0,1,2:T(8,128)(2,1)S(1)} %convert_element_type.131), channel_id=1, source_target_pairs={{0,8},{8,16},{16,24},{24,32},{32,40},{40,48},{48,56},{56,64},{64,7... | collective-permute-start | bytes 589832 | tf_op jit(solution)/shard_map/while/body/eval_jaxpr/ppermute | solution.py:9
  441.2 10.7 %collective-permute-start = (bf16[128,2,3,128]{3,0,1,2:T(8,128)(2,1)S(1)}, bf16[128,2,3,128]{3,0,1,2:T(8,128)(2,1)S(1)}, u32[]{:S(2)}, u32[]{:S(2)}) collective-permute-start(bf16[128,2,3,128]{3,0,1,2:T(8,128)(2,1)S(1)} %convert_element_type.131), channel_id=1, source_target_pairs={{0,8},{8,16},{16,24},{24,32},{32,40},{40,48},{48,56},{56,64},{64,7... | collective-permute-start | bytes 589832 | tf_op jit(solution)/shard_map/while/body/eval_jaxpr/ppermute | solution.py:9
  452.0 9.8 %collective-permute-start = (bf16[128,2,3,128]{3,0,1,2:T(8,128)(2,1)S(1)}, bf16[128,2,3,128]{3,0,1,2:T(8,128)(2,1)S(1)}, u32[]{:S(2)}, u32[]{:S(2)}) collective-permute-start(bf16[128,2,3,128]{3,0,1,2:T(8,128)(2,1)S(1)} %convert_element_type.131), channel_id=1, source_target_pairs={{0,8},{8,16},{16,24},{24,32},{32,40},{40,48},{48,56},{56,64},{64,7... | collective-permute-start | bytes 589832 | tf_op jit(solution)/shard_map/while/body/eval_jaxpr/ppermute | solution.py:9
  461.9 9.0 %collective-permute-start = (bf16[128,2,3,128]{3,0,1,2:T(8,128)(2,1)S(1)}, bf16[128,2,3,128]{3,0,1,2:T(8,128)(2,1)S(1)}, u32[]{:S(2)}, u32[]{:S(2)}) collective-permute-start(bf16[128,2,3,128]{3,0,1,2:T(8,128)(2,1)S(1)} %convert_element_type.131), channel_id=1, source_target_pairs={{0,8},{8,16},{16,24},{24,32},{32,40},{40,48},{48,56},{56,64},{64,7... | collective-permute-start | bytes 589832 | tf_op jit(solution)/shard_map/while/body/eval_jaxpr/ppermute | solution.py:9
  471.0 8.8 %collective-permute-start = (bf16[128,2,3,128]{3,0,1,2:T(8,128)(2,1)S(1)}, bf16[128,2,3,128]{3,0,1,2:T(8,128)(2,1)S(1)}, u32[]{:S(2)}, u32[]{:S(2)}) collective-permute-start(bf16[128,2,3,128]{3,0,1,2:T(8,128)(2,1)S(1)} %convert_element_type.131), channel_id=1, source_target_pairs={{0,8},{8,16},{16,24},{24,32},{32,40},{40,48},{48,56},{56,64},{64,7... | collective-permute-start | bytes 589832 | tf_op jit(solution)/shard_map/while/body/eval_jaxpr/ppermute | solution.py:9
  479.9 8.8 %collective-permute-start = (bf16[128,2,3,128]{3,0,1,2:T(8,128)(2,1)S(1)}, bf16[128,2,3,128]{3,0,1,2:T(8,128)(2,1)S(1)}, u32[]{:S(2)}, u32[]{:S(2)}) collective-permute-start(bf16[128,2,3,128]{3,0,1,2:T(8,128)(2,1)S(1)} %convert_element_type.131), channel_id=1, source_target_pairs={{0,8},{8,16},{16,24},{24,32},{32,40},{40,48},{48,56},{56,64},{64,7... | collective-permute-start | bytes 589832 | tf_op jit(solution)/shard_map/while/body/eval_jaxpr/ppermute | solution.py:9
  488.7 8.8 %collective-permute-start = (bf16[128,2,3,128]{3,0,1,2:T(8,128)(2,1)S(1)}, bf16[128,2,3,128]{3,0,1,2:T(8,128)(2,1)S(1)}, u32[]{:S(2)}, u32[]{:S(2)}) collective-permute-start(bf16[128,2,3,128]{3,0,1,2:T(8,128)(2,1)S(1)} %convert_element_type.131), channel_id=1, source_target_pairs={{0,8},{8,16},{16,24},{24,32},{32,40},{40,48},{48,56},{56,64},{64,7... | collective-permute-start | bytes 589832 | tf_op jit(solution)/shard_map/while/body/eval_jaxpr/ppermute | solution.py:9
  497.6 8.8 %collective-permute-start = (bf16[128,2,3,128]{3,0,1,2:T(8,128)(2,1)S(1)}, bf16[128,2,3,128]{3,0,1,2:T(8,128)(2,1)S(1)}, u32[]{:S(2)}, u32[]{:S(2)}) collective-permute-start(bf16[128,2,3,128]{3,0,1,2:T(8,128)(2,1)S(1)} %convert_element_type.131), channel_id=1, source_target_pairs={{0,8},{8,16},{16,24},{24,32},{32,40},{40,48},{48,56},{56,64},{64,7... | collective-permute-start | bytes 589832 | tf_op jit(solution)/shard_map/while/body/eval_jaxpr/ppermute | solution.py:9
  506.5 8.8 %collective-permute-start = (bf16[128,2,3,128]{3,0,1,2:T(8,128)(2,1)S(1)}, bf16[128,2,3,128]{3,0,1,2:T(8,128)(2,1)S(1)}, u32[]{:S(2)}, u32[]{:S(2)}) collective-permute-start(bf16[128,2,3,128]{3,0,1,2:T(8,128)(2,1)S(1)} %convert_element_type.131), channel_id=1, source_target_pairs={{0,8},{8,16},{16,24},{24,32},{32,40},{40,48},{48,56},{56,64},{64,7... | collective-permute-start | bytes 589832 | tf_op jit(solution)/shard_map/while/body/eval_jaxpr/ppermute | solution.py:9
  517.2 36.6 %all-to-all-start.1 = ((bf16[4,2,64,256]{3,2,1,0:T(8,128)(2,1)}), bf16[4,2,64,256]{3,2,1,0:T(8,128)(2,1)S(1)}, u32[]{:S(2)}, u32[]{:S(2)}) async-start(bf16[4,2,64,256]{3,2,1,0:T(8,128)(2,1)} %copy.34), calls=%async_computation.2 | async-start | bytes 524288 | tf_op jit(solution)/shard_map/all_to_all | solution.py:86
  553.8 50.9 %all-to-all-start.3 = ((bf16[4,2,64,256]{3,2,1,0:T(8,128)(2,1)}), bf16[4,2,64,256]{3,2,1,0:T(8,128)(2,1)S(1)}, u32[]{:S(2)}, u32[]{:S(2)}) async-start(bf16[4,2,64,256]{3,2,1,0:T(8,128)(2,1)} %copy.37), calls=%async_computation.5 | async-start | bytes 524288 | tf_op jit(solution)/shard_map/all_to_all | solution.py:87
  (8 other events, 220.9 us)
Sparse Core Ops, SparseCore 0:
  10.1 75.4 all-gather.9
  88.7 65.0 all-gather.5
  155.9 70.5 all-gather.7
  228.4 69.2 all-gather.11
  300.6 64.0 all-gather.13
  369.5 88.7 reduce-scatter.2
  462.9 89.1 reduce-scatter.4
where the time goes:
time: 616 us; the launch traced here: 615 us
  waiting for transfers between devices  437 us (71%)
  blocking collectives  57.6 us (9%)
  matrix products  40.6 us (7%)
  starting transfers between devices  38.3 us (6%)
  local copies, waits for them, and re-layouts  18 us (3%)
  between operations  14.4 us (2%)
  other arithmetic  7.86 us (1%)
    ppermute x15, waiting for transfers between devices, shifted(): lax.ppermute(x, axis, [(i, (i + by) % devices) for i in range(devices)])  81.7 us
    all_gather x1, waiting for transfers between devices, body(): lax.all_gather(w_gate, 'blk', axis=1, tiled=True)  69.3 us
    all_gather x1, waiting for transfers between devices, body(): lax.all_gather(w_down, 'blk', axis=2, tiled=True)  68.5 us
    all_gather x1, waiting for transfers between devices, body(): lax.all_gather(token_recv, 'local', axis=3, tiled=True)  68.1 us
    all_gather x1, waiting for transfers between devices, body(): lax.all_gather(grad_recv, 'local', axis=3, tiled=True)  67 us
    all_gather x1, waiting for transfers between devices, body(): lax.all_gather(w_up, 'blk', axis=1, tiled=True)  49.2 us
    psum x1, blocking collectives, body(): grad_gates = lax.psum(gate_terms, 'local')  41.6 us
    reduce_scatter x1, waiting for transfers between devices, body(): lax.psum_scatter(input_terms.astype(jnp.bfloat16), 'local', scatter_dimen...  30.8 us
  transfers between devices with their start and end apart: 24, of which 21 were waited for; matrix products, arithmetic and copies ran while one was open for 9% of the time, Pallas kernels for 0%

commit v1 on v0

v1 whole, which is shorter than its diff:
```python
import jax
import jax.numpy as jnp
from jax import lax
from jax.sharding import PartitionSpec as P

PLANE = ("group", "local")


def gather_rows(x):
    full = lax.all_gather(x, PLANE, axis=0, tiled=False)
    groups = lax.axis_size("group")
    full = full.reshape(groups, -1, x.shape[0], x.shape[1])
    return jnp.transpose(full, (0, 2, 1, 3)).reshape(groups * x.shape[0], -1)


def scatter_rows(x, rows, cols):
    groups = lax.axis_size("group")
    parts = x.reshape(groups, rows, -1, cols)
    parts = jnp.transpose(parts, (0, 2, 1, 3)).reshape(-1, rows, cols)
    return lax.psum_scatter(parts, PLANE, scatter_dimension=0, tiled=True)[0]


def body(tokens, d_out, ids, gates, w_gate, w_up, w_down):
    f32, bf16 = jnp.float32, jnp.bfloat16
    rows, cols = tokens.shape
    own = w_gate.shape[0]
    toks = gather_rows(tokens)
    douts = gather_rows(d_out)
    all_ids = lax.all_gather(ids, "group", axis=0, tiled=True)
    all_gates = lax.all_gather(gates, "group", axis=0, tiled=True)
    gate_full = lax.all_gather(w_gate, "blk", axis=1, tiled=True)
    up_full = lax.all_gather(w_up, "blk", axis=1, tiled=True)
    down_full = lax.all_gather(w_down, "blk", axis=2, tiled=True)
    mine = lax.axis_index("group") * own + jnp.arange(own, dtype=jnp.int32)
    chosen = all_ids[:, :, None] == mine[None, None, :]
    weight = jnp.sum(jnp.where(chosen, all_gates[:, :, None], 0.0), axis=1)
    routed = jnp.any(chosen, axis=1).astype(f32)
    pre_gate = jnp.einsum("td,edf->tef", toks, gate_full, preferred_element_type=f32)
    pre_up = jnp.einsum("td,edf->tef", toks, up_full, preferred_element_type=f32)
    back = jnp.einsum("td,efd->tef", douts, down_full, preferred_element_type=f32)
    s = jax.nn.sigmoid(pre_gate)
    hidden = pre_gate * s * pre_up
    weighted = (weight[:, :, None] * hidden).astype(bf16)
    d_hidden = weight[:, :, None] * back
    d_gate = (d_hidden * pre_up * s * (1.0 + pre_gate * (1.0 - s))).astype(bf16)
    d_up = (d_hidden * pre_gate * s).astype(bf16)
    pair = jnp.sum(hidden * back, axis=2)
    pair = jnp.sum(jnp.where(chosen, pair[:, None, :], 0.0), axis=2)
    grad_gates = lax.psum(pair, PLANE)
    grad_gates = lax.dynamic_slice_in_dim(grad_gates, lax.axis_index("group") * rows, rows, 0)
    out = jnp.einsum("tef,efd->td", weighted, down_full, preferred_element_type=f32)
    back_in = jnp.einsum("tef,edf->td", d_gate, gate_full, preferred_element_type=f32)
    back_in = back_in + jnp.einsum("tef,edf->td", d_up, up_full, preferred_element_type=f32)
    moe_out = scatter_rows(out.astype(bf16), rows, cols)
    grad_tokens = scatter_rows(back_in.astype(bf16), rows, cols)
    g_gate = jnp.einsum("td,tef->edf", toks, d_gate, preferred_element_type=f32).astype(bf16)
    g_up = jnp.einsum("td,tef->edf", toks, d_up, preferred_element_type=f32).astype(bf16)
    g_down = jnp.einsum("tef,td->efd", weighted, douts, preferred_element_type=f32).astype(bf16)
    g_gate = lax.psum_scatter(g_gate, "blk", scatter_dimension=1, tiled=True)
    g_up = lax.psum_scatter(g_up, "blk", scatter_dimension=1, tiled=True)
    g_down = lax.psum_scatter(g_down, "blk", scatter_dimension=2, tiled=True)
    return (moe_out, grad_tokens, grad_gates, g_gate.astype(f32), g_up.astype(f32), g_down.astype(f32))


def solution(mesh):
    in_specs = (
        P(("group", "blk"), "local"),
        P(("group", "blk"), "local"),
        P(("group", "blk"), None),
        P(("group", "blk"), None),
        P("group", "blk", "local"),
        P("group", "blk", "local"),
        P("group", "local", "blk"),
    )
    out_specs = (
        P(("group", "blk"), "local"),
        P(("group", "blk"), "local"),
        P(("group", "blk"), None),
        P("group", "blk", "local"),
        P("group", "blk", "local"),
        P("group", "local", "blk"),
    )
    return jax.shard_map(body, mesh=mesh, in_specs=in_specs, out_specs=out_specs, check_vma=False)
```

time: 616 us -> 977 us (1.59)
  waiting for transfers between devices: 437 us -> 799 us
  starting transfers between devices: 38.3 us -> 0.58 us
  local copies, waits for them, and re-layouts: 18 us -> 49.2 us
  blocking collectives: 57.6 us -> 87.2 us
  matrix products: 40.6 us -> 23.1 us
    reduce_scatter x2, waiting for transfers between devices: 30.9 us -> 326 us  [scatter_rows(): return lax.psum_scatter(parts, PLANE, scatter_dimension=0, tiled=True)[0]]
    unnamed x7 -> x13, waiting for transfers between devices: 1.95 us -> 103 us
    ppermute x15 -> x0, waiting for transfers between devices: 81.7 us -> none  [shifted(): lax.ppermute(x, axis, [(i, (i + by) % devices) for i in range(devices)])]
    all_gather x5, waiting for transfers between devices: 322 us -> 370 us  [the longest x2 176 us: gather_rows(): full = lax.all_gather(x, PLANE, axis=0, tiled=False)]
    psum x1, blocking collectives: 41.6 us -> 76.6 us  [body(): grad_gates = lax.psum(pair, PLANE)]
    ppermute x15 -> x0, starting transfers between devices: 30.3 us -> none  [shifted(): lax.ppermute(x, axis, [(i, (i + by) % devices) for i in range(devices)])]
    dot_general x54 -> x7, matrix products: 40.6 us -> 15 us  [the longest x1 4.72 us: body(): jnp.einsum('td,efd->tef', douts, down_full, preferred_element_type=f32)]
    unnamed x19 -> x37, local copies, waits for them, and re-layouts: 2.9 us -> 24.8 us
  transfers between devices with their start and end apart: 24 -> 10, of which waited for: 21 -> 9; matrix products, arithmetic and copies ran while one was open for 9% -> 6% of each run, Pallas kernels for 0% -> 0%
where the time goes in v1:
time: 977 us; the launch traced here: 976 us
  waiting for transfers between devices  799 us (82%)
  blocking collectives  87.2 us (9%)
  local copies, waits for them, and re-layouts  49.2 us (5%)
  matrix products  23.1 us (2%)
  between operations  14.4 us (1%)
    reduce_scatter x2, waiting for transfers between devices, scatter_rows(): return lax.psum_scatter(parts, PLANE, scatter_dimension=0, tiled=True)[0]  326 us
    all_gather x2, waiting for transfers between devices, gather_rows(): full = lax.all_gather(x, PLANE, axis=0, tiled=False)  176 us
    unnamed x13, waiting for transfers between devices  103 us
    psum x1, blocking collectives, body(): grad_gates = lax.psum(pair, PLANE)  76.6 us
    all_gather x1, waiting for transfers between devices, body(): gate_full = lax.all_gather(w_gate, 'blk', axis=1, tiled=True)  66.5 us
    all_gather x1, waiting for transfers between devices, body(): down_full = lax.all_gather(w_down, 'blk', axis=2, tiled=True)  65.9 us
    all_gather x1, waiting for transfers between devices, body(): up_full = lax.all_gather(w_up, 'blk', axis=1, tiled=True)  61.7 us
    unnamed x37, local copies, waits for them, and re-layouts  24.8 us
  transfers between devices with their start and end apart: 10, of which 9 were waited for; matrix products, arithmetic and copies ran while one was open for 6% of the time, Pallas kernels for 0%

profile of v1, /device:TPU:6, one launch (start us, length us, event | category | flops | bytes accessed | tf_op | source)
XLA Modules:
  0.0 976.3 jit_solution(13472181736398152190)
XLA Ops:
  12.6 5.3 all-gather.2
  18.0 5.3 all-gather.3
  23.4 84.1 %all-gather.16.cloned.1.call-done = bf16[6144,256]{1,0:T(8,128)(2,1)} async-done(((bf16[192,256]{1,0:T(8,128)(2,1)}), bf16[6144,256]{1,0:T(8,128)(2,1)}) %all-gather.16.cloned.1.call-update) | async-done | bytes 3145744 | tf_op jit(solution)/shard_map/all_gather | solution.py:10
  107.5 3.7 copy.103
  111.2 92.2 %all-gather.18.cloned.1.call-done = bf16[6144,256]{1,0:T(8,128)(2,1)} async-done(((bf16[192,256]{1,0:T(8,128)(2,1)}), bf16[6144,256]{1,0:T(8,128)(2,1)}) %all-gather.18.cloned.1.call-update) | async-done | bytes 3145744 | tf_op jit(solution)/shard_map/all_gather | solution.py:10
  203.4 5.4 copy.99
  208.7 5.9 reshape.65
  214.6 2.8 copy.87
  217.4 61.7 %all-gather.12.cloned.1.call-done = bf16[2,2048,128]{1,2,0:T(8,128)(2,1)} async-done(((bf16[2,128,128]{1,2,0:T(8,128)(2,1)}), bf16[2,2048,128]{1,2,0:T(8,128)(2,1)}) %all-gather.12.cloned.1.call-update) | async-done | bytes 1048592 | tf_op jit(solution)/shard_map/all_gather | solution.py:32
  279.1 4.1 fusion.6
  283.2 66.5 %all-gather.10.cloned.1.call-done = bf16[2,2048,128]{1,2,0:T(8,128)(2,1)} async-done(((bf16[2,128,128]{1,2,0:T(8,128)(2,1)}), bf16[2,2048,128]{1,2,0:T(8,128)(2,1)}) %all-gather.10.cloned.1.call-update) | async-done | bytes 1048592 | tf_op jit(solution)/shard_map/all_gather | solution.py:31
  349.7 4.1 fusion.5
  353.7 65.9 %all-gather.14.cloned.1.call-done = bf16[2,128,2048]{2,1,0:T(8,128)(2,1)} async-done(((bf16[2,128,128]{2,1,0:T(8,128)(2,1)}), bf16[2,128,2048]{2,1,0:T(8,128)(2,1)}) %all-gather.14.cloned.1.call-update) | async-done | bytes 1048592 | tf_op jit(solution)/shard_map/all_gather | solution.py:33
  419.7 4.7 multiply_reduce_fusion
  426.6 3.7 copy.85
  432.9 3.5 reshape.68
  441.9 2.9 fusion.1
  451.0 2.5 copy.67
  458.1 2.4 copy.73
  460.5 76.6 %psum.7 = f32[768,2]{0,1:T(2,128)S(1)} all-reduce(f32[768,2]{0,1:T(2,128)S(1)} %get-tuple-element.30), channel_id=1, replica_groups=mesh['group'=4,'blk'=16,'local'=8] {'group','local'}, use_global_device_ids=true, to_apply=%region_5.6 | all-reduce | flops 1536 | bytes 12288 | tf_op jit(solution)/shard_map/psum | solution.py:49
  539.4 30.8 %reduce-scatter.18.cloned.1.call-done = bf16[128,256]{1,0:T(8,128)(2,1)} async-done(((bf16[2048,256]{1,0:T(8,128)(2,1)}), bf16[128,256]{1,0:T(8,128)(2,1)}) %reduce-scatter.18.cloned.1.call-update) | async-done | bytes 65552
  571.2 70.1 %reduce-scatter.16.cloned.1.call-done = bf16[128,256]{1,0:T(8,128)(2,1)} async-done(((bf16[2048,256]{1,0:T(8,128)(2,1)}), bf16[128,256]{1,0:T(8,128)(2,1)}) %reduce-scatter.16.cloned.1.call-update) | async-done | bytes 65552
  643.9 161.0 %reduce-scatter.12.cloned.1.call-done = bf16[1,192,256]{2,1,0:T(8,128)(2,1)} async-done(((bf16[32,192,256]{2,1,0:T(8,128)(2,1)}), bf16[1,192,256]{2,1,0:T(8,128)(2,1)}) %reduce-scatter.12.cloned.1.call-update) | async-done | bytes 98320 | tf_op jit(solution)/shard_map/reduce_scatter | solution.py:20
  804.9 164.6 %reduce-scatter.14.cloned.1.call-done = bf16[1,192,256]{2,1,0:T(8,128)(2,1)} async-done(((bf16[32,192,256]{2,1,0:T(8,128)(2,1)}), bf16[1,192,256]{2,1,0:T(8,128)(2,1)}) %reduce-scatter.14.cloned.1.call-update) | async-done | bytes 98320 | tf_op jit(solution)/shard_map/reduce_scatter | solution.py:20
  (70 shorter events, 32.3 us)
Async XLA Ops:
  7.2 100.3 %all-gather.16.cloned.1.call-start = ((), (), s32[]{:S(2)}) async-start(), calls=%async_computation.10 | async-start | bytes 3244032 | tf_op jit(solution)/shard_map/all_gather | solution.py:10
  7.9 195.5 %all-gather.18.cloned.1.call-start = ((), (), s32[]{:S(2)}) async-start(), calls=%async_computation.11 | async-start | bytes 3244032 | tf_op jit(solution)/shard_map/all_gather | solution.py:10
  8.6 270.4 %all-gather.12.cloned.1.call-start = ((), (), s32[]{:S(2)}) async-start(), calls=%async_computation.6 | async-start | bytes 1114112 | tf_op jit(solution)/shard_map/all_gather | solution.py:32
  10.3 339.4 %all-gather.10.cloned.1.call-start = ((), (), s32[]{:S(2)}) async-start(), calls=%async_computation.5 | async-start | bytes 1114112 | tf_op jit(solution)/shard_map/all_gather | solution.py:31
  11.9 407.7 %all-gather.14.cloned.1.call-start = ((), (), s32[]{:S(2)}) async-start(), calls=%async_computation.7 | async-start | bytes 1114112 | tf_op jit(solution)/shard_map/all_gather | solution.py:33
  12.5 525.2 %reduce-scatter.20.cloned.1.call-start = ((), (), s32[]{:S(2)}) async-start(), calls=%async_computation.14 | async-start | bytes 1114112
  419.7 4.8 copy-start
  419.7 4.8 copy-start.4
  419.7 4.8 copy-start.6
  432.6 137.6 %reduce-scatter.18.cloned.1.call-start = ((), (), s32[]{:S(2)}) async-start(), calls=%async_computation.13 | async-start | bytes 1114112
  436.3 2.6 copy-start.1
  441.9 199.5 %reduce-scatter.16.cloned.1.call-start = ((), (), s32[]{:S(2)}) async-start(), calls=%async_computation.12 | async-start | bytes 1114112
  445.6 1.3 copy-start.5
  445.6 1.7 copy-start.7
  446.8 358.1 %reduce-scatter.12.cloned.1.call-start = ((), (), s32[]{:S(2)}) async-start(), calls=%async_computation.8 | async-start | bytes 3244032 | tf_op jit(solution)/shard_map/reduce_scatter | solution.py:20
  453.5 1.2 copy-start.2
  453.5 2.2 copy-start.3
  453.5 515.9 %reduce-scatter.14.cloned.1.call-start = ((), (), s32[]{:S(2)}) async-start(), calls=%async_computation.9 | async-start | bytes 3244032 | tf_op jit(solution)/shard_map/reduce_scatter | solution.py:20
Sparse Core Ops, SparseCore 0:
  10.1 97.3 all-gather.15
  109.6 93.7 all-gather.17
  205.9 73.0 all-gather.11
  281.5 68.1 all-gather.9
  351.5 68.1 all-gather.13
  432.8 66.3 reduce-scatter.19
  502.2 68.0 reduce-scatter.17
  573.1 68.2 reduce-scatter.15
  645.0 159.8 reduce-scatter.11
  808.1 161.2 reduce-scatter.13

commit v2 on v1

v2 whole, which is shorter than its diff:
```python
import jax
import jax.numpy as jnp
from jax import lax
from jax.experimental import pallas as pl
from jax.experimental.pallas import tpu as pltpu
from jax.sharding import PartitionSpec as P

F32, BF16 = jnp.float32, jnp.bfloat16
MESH = pl.DeviceIdType.MESH
RX = RY = 4
RZ = 16
ROWS, COLS, HALF = 192, 256, 128
TOK = 768
HID = 768
CHUNK = 384
NSEM = 230


def nt(a, b):
    return lax.dot_general(a, b, (((1,), (1,)), ((), ())), preferred_element_type=F32)


def nn(a, b):
    return jnp.dot(a, b, preferred_element_type=F32)


def side(d):
    return 0 if d == 1 else 1


def gather_chunks(s, d):
    return (0, 1) if s < RZ // 2 else ((0,) if d == 1 else (1,))


def sum_chunks(s, d):
    return (0, 1) if s > 1 else ((0,) if d == 1 else (1,))


def kernel(
    tok_ref, dout_ref, wg_ref, wu_ref, wd_ref, wt_ref,
    moe_ref, gtok_ref, gg_ref, gu_ref, gd_ref, pair_ref,
    tk, wall, acc, dct, am, term, own, zs, zr, ss, sr, op, s1h, r1h, s1f, r1f, op2,
    s2h, r2h, s2f, r2f, wb, wbr, pb, pbr, ssem, rsem,
):
    g, z, l = lax.axis_index("group"), lax.axis_index("blk"), lax.axis_index("local")
    x = lax.div(l, 4) * 2 + lax.div(g, 2)
    y, c = lax.rem(l, 4), lax.rem(g, 2)

    def place(xx, yy, cc, zz):
        return (lax.rem(xx, 2) * 2 + cc, zz, lax.div(xx, 2) * 4 + yy)

    def dev(dx=0, dy=0, dz=0, other=False):
        return place(
            lax.rem(x + dx + RX, RX), lax.rem(y + dy + RY, RY), 1 - c if other else c, lax.rem(z + dz + RZ, RZ)
        )

    sibling = dev(other=True)
    zpos = lambda by: lax.rem(z + by + 2 * RZ, RZ)
    numbers, sent = {}, []

    def number(key):
        return numbers.setdefault(key, len(numbers))

    def put(key, src, dst, to):
        i = number(key)
        made = pltpu.make_async_remote_copy(
            src_ref=src, dst_ref=dst, send_sem=ssem.at[i], recv_sem=rsem.at[i], device_id=to, device_id_type=MESH
        )
        made.start()
        sent.append(made)

    def got(key, dst):
        i = number(key)
        pltpu.make_async_remote_copy(
            src_ref=dst, dst_ref=dst, send_sem=ssem.at[i], recv_sem=rsem.at[i], device_id=sibling, device_id_type=MESH
        ).wait_recv()

    for a in range(2):
        for i in range(16):
            number(("ss", a, i))

    barrier = pltpu.get_barrier_semaphore()
    near = [sibling, dev(dx=1), dev(dx=-1), dev(dx=2), dev(dy=1), dev(dy=-1), dev(dy=2), dev(dz=1), dev(dz=-1)]
    for to in near:
        pl.semaphore_signal(barrier, inc=1, device_id=to, device_id_type=MESH)

    def along(axis, d):
        return dev(dx=d) if axis == 0 else dev(dy=d)

    def rel(a, o1, o2):
        return (o1, o2) if a == 0 else (o2, o1)

    def spot(ox, oy, cc):
        xx, yy = lax.rem(x + ox + RX, RX), lax.rem(y + oy + RY, RY)
        return lax.div(xx, 2) * 4 + yy, pl.multiple_of((lax.rem(xx, 2) * 2 + cc) * ROWS, 64)

    def block(a, o, cc=None):
        ll, row = spot(*o, c if cc is None else cc)
        return tk.at[a, pl.ds(2 * ll, 2), pl.ds(row, ROWS), :]

    def half(a, o, h):
        ll, row = spot(*o, c)
        return tk.at[a, 2 * ll + h, pl.ds(row, ROWS), :]

    row = pl.multiple_of(g * ROWS, 64)
    for e in range(2):
        wall[z, e * 128 : (e + 1) * 128, :] = wg_ref[e].T
        wall[z, 256 + e * 128 : 256 + (e + 1) * 128, :] = wu_ref[e].T
        wall[z, 512 + e * 128 : 512 + (e + 1) * 128, :] = wd_ref[e]
    for a, ref in enumerate((tok_ref, dout_ref)):
        for h in range(2):
            tk[a, 2 * l + h, pl.ds(row, ROWS), :] = ref[:, h * HALF : (h + 1) * HALF]
    wb[0] = wt_ref[...]
    pb[0] = jnp.zeros((8, TOK), F32)
    pl.semaphore_wait(barrier, len(near))

    def wblock(b, ch):
        return wall.at[b, pl.ds(ch * CHUNK, CHUNK), :]

    for ch in range(2):
        for d in (1, -1):
            put(("w", 1, d, ch), wblock(z, ch), wblock(z, ch), dev(dz=d))
    for a in range(2):
        for d in (1, -1):
            put(("g1", a, d), block(a, (0, 0)), block(a, (0, 0)), along(a, d))
    for a in range(2):
        for d in (1, -1):
            put(("g2", a, 0, d), block(a, (0, 0)), block(a, (0, 0)), along(1 - a, d))
    put(("wt", 0), wb.at[0], wbr.at[0], sibling)
    for a in range(2):
        put(("gs", a, 0, 0), block(a, (0, 0)), block(a, (0, 0)), sibling)

    def column(a, o1):
        o = rel(a, o1, 0)
        for d in (1, -1):
            put(("g2", a, o1, d), block(a, o), block(a, o), along(1 - a, d))
        put(("gs", a, o1, 0), block(a, o), block(a, o), sibling)

    def first(a):
        for d in (1, -1):
            o, h = rel(a, -d, 0), side(d)
            got(("g1", a, d), block(a, o))
            put(("g1h", a, d), half(a, o, h), half(a, o, h), along(a, d))
        for d in (1, -1):
            column(a, -d)

    def opposite(a):
        for d in (1, -1):
            got(("g1h", a, d), half(a, rel(a, 2, 0), side(d)))
        column(a, 2)

    def second(a, o1):
        for d in (1, -1):
            o, h = rel(a, o1, -d), side(d)
            got(("g2", a, o1, d), block(a, o))
            put(("g2h", a, o1, d), half(a, o, h), half(a, o, h), along(1 - a, d))
            put(("gs", a, o1, -d), block(a, o), block(a, o), sibling)

    def across(a, o1):
        o = rel(a, o1, 2)
        for d in (1, -1):
            got(("g2h", a, o1, d), half(a, o, side(d)))
        put(("gs", a, o1, 2), block(a, o), block(a, o), sibling)

    def from_sibling(a):
        for o1 in (0, 1, -1, 2):
            for o2 in (0, 1, -1, 2):
                got(("gs", a, o1, o2), block(a, rel(a, o1, o2), 1 - c))

    def weights(s):
        for ch in range(2):
            for d in (1, -1):
                if ch not in gather_chunks(s, d):
                    continue
                where = wblock(zpos(-d * s), ch)
                got(("w", s, d, ch), where)
                if s < RZ // 2 and ch in gather_chunks(s + 1, d):
                    put(("w", s + 1, d, ch), where, where, dev(dz=d))

    def project(b1, b2, fresh=False):
        def tile(t, carry):
            rows = pl.ds(pl.multiple_of(t * 256, 256), 256)
            for a, lo, hi in ((0, 0, 512), (1, 512, 768)):
                lhs = jnp.concatenate([wall[b1, lo:hi, :], wall[b2, lo:hi, :]], axis=1)
                rhs = jnp.concatenate([tk[a, b1, rows, :], tk[a, b2, rows, :]], axis=1)
                value = nt(lhs, rhs)
                acc[t, lo:hi, :] = value if fresh else acc[t, lo:hi, :] + value
            return carry

        lax.fori_loop(0, 3, tile, 0)

    first(0)
    first(1)
    weights(1)
    second(0, 0)
    second(1, 0)
    got(("wt", 0), wbr.at[0])
    wb[1] = wb[0] + wbr[0]
    near_x = place(x + 1 - 2 * lax.rem(x, 2), y, c, z)
    put(("wt", 1), wb.at[1], wbr.at[1], near_x)
    opposite(0)
    opposite(1)
    weights(2)
    for o1 in (-1, 1):
        second(0, o1)
        second(1, o1)
    weights(3)
    for o1 in (0, -1):
        across(0, o1)
        across(1, o1)
    second(0, 2)
    second(1, 2)
    weights(4)
    for o1 in (1, 2):
        across(0, o1)
        across(1, o1)
    got(("wt", 1), wbr.at[1])
    wb[2] = wb[1] + wbr[1]
    from_sibling(0)
    from_sibling(1)
    project(zpos(1), zpos(-1), True)
    project(zpos(2), zpos(-2))
    weights(5)
    project(zpos(3), zpos(-3))
    project(zpos(4), zpos(-4))
    weights(6)
    project(zpos(5), zpos(-5))
    project(zpos(6), zpos(-6))
    weights(7)
    project(zpos(7), zpos(-7))
    weights(8)
    project(z, zpos(8))

    for t in range(3):
        for e in range(2):
            f = slice(e * 128, (e + 1) * 128)
            gate = acc[t, f, :]
            up = acc[t, 256 + e * 128 : 256 + (e + 1) * 128, :]
            back = acc[t, 512 + e * 128 : 512 + (e + 1) * 128, :]
            weight = wb[2, pl.ds(2 * g + e, 1), t * 256 : (t + 1) * 256]
            s = jax.nn.sigmoid(gate)
            hidden = gate * s * up
            d_hidden = weight * back
            dct[t, f, :] = (d_hidden * up * s * (1.0 + gate * (1.0 - s))).astype(BF16)
            dct[t, 256 + e * 128 : 256 + (e + 1) * 128, :] = (d_hidden * gate * s).astype(BF16)
            dct[t, 512 + e * 128 : 512 + (e + 1) * 128, :] = (weight * hidden).astype(BF16)
            pair = jnp.sum(hidden * back, axis=0, keepdims=True)
            pb[0, pl.ds(2 * g + e, 1), t * 256 : (t + 1) * 256] = jnp.where(weight > 0, pair, 0.0)

    def products(b1, b2):
        for a, lo, hi in ((0, 0, 512), (1, 512, 768)):
            total = None
            for t in range(3):
                rhs = jnp.concatenate(
                    [tk[a, b1, t * 256 : (t + 1) * 256, :], tk[a, b2, t * 256 : (t + 1) * 256, :]], axis=1
                )
                value = nn(dct[t, lo:hi, :], rhs)
                total = value if total is None else total + value
            term[lo:hi, :] = total

    def pass_on(s):
        products(zpos(9 - s), z if s == 1 else zpos(s - 9))
        if s == 1:
            own[...] = term[:, 128:]
        for ch in range(2):
            rows = slice(ch * CHUNK, (ch + 1) * CHUNK)
            for d in (1, -1):
                k = side(d)
                if ch not in sum_chunks(s, d):
                    continue
                lanes = slice(0, 128) if s == 1 else slice(k * 128, (k + 1) * 128)
                value = term[rows, lanes]
                if s > 1 and ch in sum_chunks(s - 1, d):
                    got(("r", s - 1, d, ch), zr.at[k, s - 2, rows, :])
                    value = value + zr[k, s - 2, rows, :].astype(F32)
                zs[k, s - 1, rows, :] = value.astype(BF16)
                put(("r", s, d, ch), zs.at[k, s - 1, rows, :], zr.at[k, s - 1, rows, :], dev(dz=d))

    def partials(dx):
        def one(dy, carry):
            i = (dx % 4) * 4 + dy
            xx, yy = lax.rem(x + dx + RX, RX), lax.rem(y + dy, RY)
            ll = lax.div(xx, 2) * 4 + yy
            base = lax.rem(xx, 2) * 2
            mine = pl.multiple_of((base + c) * ROWS, 64)
            theirs = pl.multiple_of((base + 1 - c) * ROWS, 64)
            lhs = jnp.concatenate([am[pl.ds(mine, ROWS), :], am[pl.ds(theirs, ROWS), :]], axis=0)
            for a, lo, hi in ((0, 512, 768), (1, 0, 512)):
                rhs = jnp.concatenate([wall[2 * ll, lo:hi, :], wall[2 * ll + 1, lo:hi, :]], axis=1)
                value = nn(lhs[:, lo:hi], rhs)
                op[a, i] = value[:ROWS]
                ss[a, i] = value[ROWS:].astype(BF16)
                k = a * 16 + i
                pltpu.make_async_remote_copy(
                    src_ref=ss.at[a, i], dst_ref=sr.at[a, i], send_sem=ssem.at[k], recv_sem=rsem.at[k],
                    device_id=sibling, device_id_type=MESH,
                ).start()
            return carry

        lax.fori_loop(0, 4, one, 0)

    def whole(a, o1, o2):
        ox, oy = rel(a, o1, o2)
        i = (ox % 4) * 4 + oy % 4
        got(("ss", a, i), sr.at[a, i])
        return op[a, i] + sr[a, i].astype(F32)

    def far(a, o2):
        value = whole(a, 2, o2).astype(BF16)
        for d in (1, -1):
            k = side(d)
            s1h[a, k, o2] = value[:, k * HALF : (k + 1) * HALF]
            put(("p1h", a, o2, d), s1h.at[a, k, o2], r1h.at[a, k, o2], along(a, d))

    def next_to(a, o2):
        for d in (1, -1):
            k = side(d)
            value = whole(a, d, o2)
            got(("p1h", a, o2, d), r1h.at[a, k, o2])
            more = r1h[a, k, o2].astype(F32)
            for h in range(2):
                part = value[:, h * HALF : (h + 1) * HALF]
                s1f[a, k, o2, :, h * HALF : (h + 1) * HALF] = (part + more if h == k else part).astype(BF16)
            put(("p1f", a, o2, d), s1f.at[a, k, o2], r1f.at[a, k, o2], along(a, d))

    def here(a, o2):
        value = whole(a, 0, o2)
        for d in (1, -1):
            got(("p1f", a, o2, d), r1f.at[a, side(d), o2])
            value = value + r1f[a, side(d), o2].astype(F32)
        op2[a, o2] = value
        if o2 == 2:
            low = value.astype(BF16)
            for d in (1, -1):
                k = side(d)
                s2h[a, k] = low[:, k * HALF : (k + 1) * HALF]
                put(("p2h", a, d), s2h.at[a, k], r2h.at[a, k], along(1 - a, d))

    def turn(a):
        for d in (1, -1):
            k = side(d)
            got(("p2h", a, d), r2h.at[a, k])
            more = r2h[a, k].astype(F32)
            for h in range(2):
                part = op2[a, d % 4, :, h * HALF : (h + 1) * HALF]
                s2f[a, k, :, h * HALF : (h + 1) * HALF] = (part + more if h == k else part).astype(BF16)
            put(("p2f", a, d), s2f.at[a, k], r2f.at[a, k], along(1 - a, d))

    def finish(a, ref):
        value = op2[a, 0]
        for d in (1, -1):
            got(("p2f", a, d), r2f.at[a, side(d)])
            value = value + r2f[a, side(d)].astype(F32)
        ref[...] = value.astype(BF16)

    partner = [
        sibling, near_x, dev(dx=2), place(x, y + 1 - 2 * lax.rem(y, 2), c, z), dev(dy=2),
    ]

    def share(k):
        if k:
            got(("p", k - 1), pbr.at[k - 1])
            pb[k] = pb[k - 1] + pbr[k - 1]
        if k < len(partner):
            put(("p", k), pb.at[k], pbr.at[k], partner[k])
        else:
            pair_ref[...] = pb[k]

    pass_on(1)
    share(0)
    for t in range(3):
        for u in range(6):
            am[t * 256 : (t + 1) * 256, u * 128 : (u + 1) * 128] = dct[t, u * 128 : (u + 1) * 128, :].T
    pass_on(2)
    partials(2)
    share(1)
    pass_on(3)
    partials(1)
    partials(-1)
    share(2)
    partials(0)
    pass_on(4)
    for o2 in (2, 1, 3, 0):
        for a in range(2):
            far(a, o2)
    share(3)
    pass_on(5)
    for o2 in (2, 1, 3, 0):
        for a in range(2):
            next_to(a, o2)
    share(4)
    pass_on(6)
    for o2 in (2, 1, 3):
        for a in range(2):
            here(a, o2)
    share(5)
    pass_on(7)
    for a in range(2):
        here(a, 0)
        turn(a)
    pass_on(8)
    finish(0, moe_ref)
    finish(1, gtok_ref)
    for ch in range(2):
        for d in (1, -1):
            got(("r", 8, d, ch), zr.at[side(d), 7, pl.ds(ch * CHUNK, CHUNK), :])
    for e in range(2):
        for base, ref in ((0, gg_ref), (256, gu_ref), (512, gd_ref)):
            rows = slice(base + e * 128, base + (e + 1) * 128)
            value = own[rows, :] + zr[0, 7, rows, :].astype(F32) + zr[1, 7, rows, :].astype(F32)
            ref[e] = value if base == 512 else value.T

    for made in sent:
        made.wait_send()
    for a in range(2):
        for i in range(16):
            k = a * 16 + i
            pltpu.make_async_remote_copy(
                src_ref=ss.at[a, i], dst_ref=sr.at[a, i], send_sem=ssem.at[k], recv_sem=rsem.at[k],
                device_id=sibling, device_id_type=MESH,
            ).wait_send()
    assert len(numbers) <= NSEM, len(numbers)


def body(tokens, d_out, ids, gates, w_gate, w_up, w_down):
    experts = w_gate.shape[0] * lax.axis_size("group")
    place = lax.axis_index("group") * ROWS
    chosen = ids.T[:, None, :] == jnp.arange(experts, dtype=jnp.int32)[None, :, None]
    weight = jnp.sum(jnp.where(chosen, gates.T[:, None, :], 0.0), axis=0)
    weight = lax.dynamic_update_slice(jnp.zeros((experts, TOK), F32), weight, (0, place))
    vm = pl.BlockSpec(memory_space=pltpu.VMEM)
    shape = jax.ShapeDtypeStruct
    moe, gtok, gg, gu, gd, pair = pl.pallas_call(
        kernel,
        out_shape=(
            shape(tokens.shape, BF16),
            shape(tokens.shape, BF16),
            shape(w_gate.shape, F32),
            shape(w_up.shape, F32),
            shape(w_down.shape, F32),
            shape((experts, TOK), F32),
        ),
        in_specs=[vm] * 6,
        out_specs=(vm,) * 6,
        scratch_shapes=[
            pltpu.VMEM((2, 16, TOK, 128), BF16),
            pltpu.VMEM((16, HID, 128), BF16),
            pltpu.VMEM((3, HID, 256), F32),
            pltpu.VMEM((3, HID, 256), BF16),
            pltpu.VMEM((TOK, HID), BF16),
            pltpu.VMEM((HID, 256), F32),
            pltpu.VMEM((HID, 128), F32),
            pltpu.VMEM((2, 8, HID, 128), BF16),
            pltpu.VMEM((2, 8, HID, 128), BF16),
            pltpu.VMEM((2, 16, ROWS, COLS), BF16),
            pltpu.VMEM((2, 16, ROWS, COLS), BF16),
            pltpu.VMEM((2, 16, ROWS, COLS), F32),
            pltpu.VMEM((2, 2, 4, ROWS, HALF), BF16),
            pltpu.VMEM((2, 2, 4, ROWS, HALF), BF16),
            pltpu.VMEM((2, 2, 4, ROWS, COLS), BF16),
            pltpu.VMEM((2, 2, 4, ROWS, COLS), BF16),
            pltpu.VMEM((2, 4, ROWS, COLS), F32),
            pltpu.VMEM((2, 2, ROWS, HALF), BF16),
            pltpu.VMEM((2, 2, ROWS, HALF), BF16),
            pltpu.VMEM((2, 2, ROWS, COLS), BF16),
            pltpu.VMEM((2, 2, ROWS, COLS), BF16),
            pltpu.VMEM((3, 8, TOK), F32),
            pltpu.VMEM((2, 8, TOK), F32),
            pltpu.VMEM((6, 8, TOK), F32),
            pltpu.VMEM((5, 8, TOK), F32),
            pltpu.SemaphoreType.DMA((NSEM,)),
            pltpu.SemaphoreType.DMA((NSEM,)),
        ],
        compiler_params=pltpu.CompilerParams(
            collective_id=0, has_side_effects=True, vmem_limit_bytes=58 * 2**20
        ),
    )(tokens, d_out, w_gate, w_up, w_down, weight)
    pair = lax.dynamic_slice(pair, (0, place), (experts, ROWS))
    grad_gates = jnp.sum(jnp.where(chosen, pair[None, :, :], 0.0), axis=1).T
    return (moe, gtok, grad_gates, gg, gu, gd)


def solution(mesh):
    in_specs = (
        P(("group", "blk"), "local"),
        P(("group", "blk"), "local"),
        P(("group", "blk"), None),
        P(("group", "blk"), None),
        P("group", "blk", "local"),
        P("group", "blk", "local"),
        P("group", "local", "blk"),
    )
    out_specs = (
        P(("group", "blk"), "local"),
        P(("group", "blk"), "local"),
        P(("group", "blk"), None),
        P("group", "blk", "local"),
        P("group", "blk", "local"),
        P("group", "local", "blk"),
    )
    return jax.shard_map(body, mesh=mesh, in_specs=in_specs, out_specs=out_specs, check_vma=False)
```

time: 977 us -> 118 us (0.12)
  waiting for transfers between devices: 799 us -> 0 us
  Pallas kernels: 0 us -> 109 us
  blocking collectives: 87.2 us -> 0 us
  local copies, waits for them, and re-layouts: 49.2 us -> 7.42 us
  matrix products: 23.1 us -> 0 us
  between operations: 14.4 us -> 0.69 us
    all_gather x5 -> x0, waiting for transfers between devices: 370 us -> none  [the longest x2 176 us: gather_rows(): full = lax.all_gather(x, PLANE, axis=0, tiled=False)]
    reduce_scatter x2 -> x0, waiting for transfers between devices: 326 us -> none  [scatter_rows(): return lax.psum_scatter(parts, PLANE, scatter_dimension=0, tiled=True)[0]]
    pallas_call x0 -> x1, Pallas kernels: none -> 109 us  [body(): pl.pallas_call(kernel, out_shape=(shape(tokens.shape, BF16), shape(tokens...]
    unnamed x13 -> x0, waiting for transfers between devices: 103 us -> none
    psum x1 -> x0, blocking collectives: 76.6 us -> none  [body(): grad_gates = lax.psum(pair, PLANE)]
    unnamed x37 -> x19, local copies, waits for them, and re-layouts: 24.8 us -> 6.36 us
    reshape x4 -> x0, local copies, waits for them, and re-layouts: 18.4 us -> none  [the longest x2 9.35 us: gather_rows(): return jnp.transpose(full, (0, 2, 1, 3)).reshape(groups * x.shape[0], -1)]
    dot_general x7 -> x0, matrix products: 15 us -> none  [the longest x1 4.72 us: body(): jnp.einsum('td,efd->tef', douts, down_full, preferred_element_type=f32)]
  transfers between devices with their start and end apart: 10 -> 0, of which waited for: 9 -> 0; matrix products, arithmetic and copies ran while one was open for 6% -> 0% of each run, Pallas kernels for 0% -> 0%
where the time goes in v2:
time: 118 us
  Pallas kernels  109 us (92%)
  local copies, waits for them, and re-layouts  7.42 us (6%)
    pallas_call x1, Pallas kernels, body(): pl.pallas_call(kernel, out_shape=(shape(tokens.shape, BF16), shape(tokens...  109 us
    unnamed x19, local copies, waits for them, and re-layouts  6.36 us

profile of v2, /device:TPU:6, one launch (start us, length us, event | category | flops | bytes accessed | tf_op | source)
XLA Modules:
  0.0 117.8 jit_solution(9075436476420312281)
XLA Ops:
  0.6 0.0 copy-start.6
  0.6 0.0 copy-start.5
  0.7 0.7 copy-done.6
  1.3 0.0 copy-done.5
  1.3 0.3 dynamic_update_slice.3.wt_ref
  1.6 0.0 copy-start.4
  1.6 0.6 copy-done.4
  2.2 109.1 %shard_map.118 = (bf16[192,256]{1,0:T(8,128)(2,1)}, bf16[192,256]{1,0:T(8,128)(2,1)}, f32[2,128,128]{2,1,0:T(8,128)}, f32[2,128,128]{2,1,0:T(8,128)}, f32[2,128,128]{2,1,0:T(8,128)}, /*index=5*/f32[8,768]{1,0:T(8,128)}) custom-call(bf16[192,256]{1,0:T(8,128)(2,1)} %tok_ref.1, bf16[192,256]{1,0:T(8,128)(2,1)} %dout_ref.1, bf16[2,128,128]{2,1,0:T(8,128)(2,1)} %wg_ref.1, ...), custom_call_target="tpu_custom_call" | custom-call | tf_op jit(solution)/shard_map/pallas_call | solution.py:433
  111.3 0.8 constant_dynamic-slice_fusion
  112.1 0.6 select_reduce_fusion
  112.7 0.0 copy-start.3
  112.7 1.6 %copy.19 = bf16[192,256]{1,0:T(8,128)(2,1)} copy(bf16[192,256]{1,0:T(8,128)(2,1)} %get-tuple-element.24) | data formatting | bytes 196608
  114.3 0.0 copy-done.3
  114.3 0.0 copy-start.2
  114.3 0.6 copy.20
  114.9 0.3 copy-done.2
  115.2 0.0 copy-start.1
  115.2 0.7 copy.21
  115.9 0.3 copy-done.1
  116.2 0.0 copy-start
  116.2 0.7 copy.22
  116.8 0.3 copy-done
  117.1 0.7 copy.23
  (2 shorter events, 0.0 us)
Async XLA Ops:
  0.6 0.7 copy-start.6
  0.6 0.7 copy-start.5
  1.6 0.6 copy-start.4
  112.7 1.6 %copy-start.3 = (bf16[192,256]{1,0:T(8,128)(2,1)S(1)}, bf16[192,256]{1,0:T(8,128)(2,1)}, u32[]{:S(2)}) copy-start(bf16[192,256]{1,0:T(8,128)(2,1)} %get-tuple-element.25) | copy-start | bytes 294916
  114.3 0.9 copy-start.2
  115.2 1.0 copy-start.1
  116.2 1.0 copy-start

commit v3 on v2

--- a/solution.py
+++ b/solution.py
@@ -12,8 +12,9 @@
 ROWS, COLS, HALF = 192, 256, 128
 TOK = 768
 HID = 768
-CHUNK = 384
-NSEM = 230
+CHUNK = 192
+CHUNKS = 4
+NSEM = 280
 
 
 def nt(a, b):
@@ -29,15 +30,15 @@
 
 
 def gather_chunks(s, d):
-    return (0, 1) if s < RZ // 2 else ((0,) if d == 1 else (1,))
+    return (0, 1, 2, 3) if s < RZ // 2 else ((0, 1) if d == 1 else (2, 3))
 
 
 def sum_chunks(s, d):
-    return (0, 1) if s > 1 else ((0,) if d == 1 else (1,))
+    return (0, 1, 2, 3) if s > 1 else ((0, 1) if d == 1 else (2, 3))
 
 
 def kernel(
-    tok_ref, dout_ref, wg_ref, wu_ref, wd_ref, wt_ref,
+    tok_ref, dout_ref, wg_ref, wu_ref, wd_ref, ids_ref, gates_ref,
     moe_ref, gtok_ref, gg_ref, gu_ref, gd_ref, pair_ref,
     tk, wall, acc, dct, am, term, own, zs, zr, ss, sr, op, s1h, r1h, s1f, r1f, op2,
     s2h, r2h, s2f, r2f, wb, wbr, pb, pbr, ssem, rsem,
@@ -110,14 +111,18 @@
     for a, ref in enumerate((tok_ref, dout_ref)):
         for h in range(2):
             tk[a, 2 * l + h, pl.ds(row, ROWS), :] = ref[:, h * HALF : (h + 1) * HALF]
-    wb[0] = wt_ref[...]
+    number_of = lax.broadcasted_iota(jnp.int32, (8, ROWS), 0)
+    picked = [ids_ref[k : k + 1, :] == number_of for k in range(2)]
+    weights_of = jnp.where(picked[0], gates_ref[0:1, :], 0.0) + jnp.where(picked[1], gates_ref[1:2, :], 0.0)
+    for q in range(4):
+        wb[0, :, q * ROWS : (q + 1) * ROWS] = jnp.where(g == q, weights_of, 0.0)
     pb[0] = jnp.zeros((8, TOK), F32)
     pl.semaphore_wait(barrier, len(near))
 
     def wblock(b, ch):
         return wall.at[b, pl.ds(ch * CHUNK, CHUNK), :]
 
-    for ch in range(2):
+    for ch in range(CHUNKS):
         for d in (1, -1):
             put(("w", 1, d, ch), wblock(z, ch), wblock(z, ch), dev(dz=d))
     for a in range(2):
@@ -168,7 +173,7 @@
                 got(("gs", a, o1, o2), block(a, rel(a, o1, o2), 1 - c))
 
     def weights(s):
-        for ch in range(2):
+        for ch in range(CHUNKS):
             for d in (1, -1):
                 if ch not in gather_chunks(s, d):
                     continue
@@ -262,7 +267,7 @@
         products(zpos(9 - s), z if s == 1 else zpos(s - 9))
         if s == 1:
             own[...] = term[:, 128:]
-        for ch in range(2):
+        for ch in range(CHUNKS):
             rows = slice(ch * CHUNK, (ch + 1) * CHUNK)
             for d in (1, -1):
                 k = side(d)
@@ -364,7 +369,11 @@
         if k < len(partner):
             put(("p", k), pb.at[k], pbr.at[k], partner[k])
         else:
-            pair_ref[...] = pb[k]
+            mine = jnp.zeros((8, ROWS), F32)
+            for q in range(4):
+                mine = jnp.where(g == q, pb[k, :, q * ROWS : (q + 1) * ROWS], mine)
+            for j in range(2):
+                pair_ref[j : j + 1, :] = jnp.sum(jnp.where(picked[j], mine, 0.0), axis=0, keepdims=True)
 
     pass_on(1)
     share(0)
@@ -401,7 +410,7 @@
     pass_on(8)
     finish(0, moe_ref)
     finish(1, gtok_ref)
-    for ch in range(2):
+    for ch in range(CHUNKS):
         for d in (1, -1):
             got(("r", 8, d, ch), zr.at[side(d), 7, pl.ds(ch * CHUNK, CHUNK), :])
     for e in range(2):
@@ -422,12 +431,12 @@
     assert len(numbers) <= NSEM, len(numbers)
 
 
+def hand_over(*refs):
+    for src, dst in zip(refs[:6], refs[6:]):
+        dst[...] = src[...]
+
+
 def body(tokens, d_out, ids, gates, w_gate, w_up, w_down):
-    experts = w_gate.shape[0] * lax.axis_size("group")
-    place = lax.axis_index("group") * ROWS
-    chosen = ids.T[:, None, :] == jnp.arange(experts, dtype=jnp.int32)[None, :, None]
-    weight = jnp.sum(jnp.where(chosen, gates.T[:, None, :], 0.0), axis=0)
-    weight = lax.dynamic_update_slice(jnp.zeros((experts, TOK), F32), weight, (0, place))
     vm = pl.BlockSpec(memory_space=pltpu.VMEM)
     shape = jax.ShapeDtypeStruct
     moe, gtok, gg, gu, gd, pair = pl.pallas_call(
@@ -438,9 +447,9 @@
             shape(w_gate.shape, F32),
             shape(w_up.shape, F32),
             shape(w_down.shape, F32),
-            shape((experts, TOK), F32),
+            shape(gates.shape[::-1], F32),
         ),
-        in_specs=[vm] * 6,
+        in_specs=[vm] * 7,
         out_specs=(vm,) * 6,
         scratch_shapes=[
             pltpu.VMEM((2, 16, TOK, 128), BF16),
@@ -474,10 +483,16 @@
         compiler_params=pltpu.CompilerParams(
             collective_id=0, has_side_effects=True, vmem_limit_bytes=58 * 2**20
         ),
-    )(tokens, d_out, w_gate, w_up, w_down, weight)
-    pair = lax.dynamic_slice(pair, (0, place), (experts, ROWS))
-    grad_gates = jnp.sum(jnp.where(chosen, pair[None, :, :], 0.0), axis=1).T
-    return (moe, gtok, grad_gates, gg, gu, gd)
+    )(tokens, d_out, w_gate, w_up, w_down, ids.T, gates.T)
+    made = (moe, gtok, gg, gu, gd, pair)
+    moe, gtok, gg, gu, gd, pair = pl.pallas_call(
+        hand_over,
+        out_shape=tuple(shape(a.shape, a.dtype) for a in made),
+        in_specs=[vm] * 6,
+        out_specs=(vm,) * 6,
+        compiler_params=pltpu.CompilerParams(vmem_limit_bytes=58 * 2**20),
+    )(*made)
+    return (moe, gtok, pair.T, gg, gu, gd)
 
 
 def solution(mesh):

time: 118 us -> 110 us (0.932)
  local copies, waits for them, and re-layouts: 7.42 us -> 0 us
    unnamed x19 -> x0, local copies, waits for them, and re-layouts: 6.36 us -> none
    pallas_call x0 -> x1, Pallas kernels: none -> 1.95 us  [body(): pl.pallas_call(hand_over, out_shape=tuple((shape(a.shape, a.dtype) for a...]
    pallas_call x1, Pallas kernels: 109 us -> 107 us  [body(): pl.pallas_call(kernel, out_shape=(shape(tokens.shape, BF16), shape(tokens...]
where the time goes in v3:
time: 110 us
  Pallas kernels  109 us (99%)
    pallas_call x1, Pallas kernels, body(): pl.pallas_call(kernel, out_shape=(shape(tokens.shape, BF16), shape(tokens...  107 us

profile of v3, /device:TPU:6, one launch (start us, length us, event | category | flops | bytes accessed | tf_op | source)
XLA Modules:
  0.0 110.1 jit_solution(13121724524892370034)
XLA Ops:
  0.6 107.5 %shard_map.118 = (bf16[192,256]{1,0:T(8,128)(2,1)}, bf16[192,256]{1,0:T(8,128)(2,1)}, f32[2,128,128]{2,1,0:T(8,128)}, f32[2,128,128]{2,1,0:T(8,128)}, f32[2,128,128]{2,1,0:T(8,128)}, /*index=5*/f32[2,192]{1,0:T(2,128)}) custom-call(bf16[192,256]{1,0:T(8,128)(2,1)} %tok_ref.1, bf16[192,256]{1,0:T(8,128)(2,1)} %dout_ref.1, bf16[2,128,128]{2,1,0:T(8,128)(2,1)} %wg_ref.1, ...), custom_call_target="tpu_custom_call" | custom-call | tf_op jit(solution)/shard_map/pallas_call | solution.py:442
  108.1 1.9 %shard_map.119 = (bf16[192,256]{1,0:T(8,128)(2,1)}, bf16[192,256]{1,0:T(8,128)(2,1)}, f32[2,128,128]{2,1,0:T(8,128)}, f32[2,128,128]{2,1,0:T(8,128)}, f32[2,128,128]{2,1,0:T(8,128)}, /*index=5*/f32[2,192]{1,0:T(2,128)}) custom-call(bf16[192,256]{1,0:T(8,128)(2,1)} %get-tuple-element.18.refs_0_, bf16[192,256]{1,0:T(8,128)(2,1)} %get-tuple-element.19.refs_1_, ...), custom_call_target="tpu_custom_call" | custom-call | tf_op jit(solution)/shard_map/pallas_call | solution.py:488

commit v4 on v3

--- a/solution.py
+++ b/solution.py
@@ -13,7 +13,7 @@
 TOK = 768
 HID = 768
 CHUNK = 192
-CHUNKS = 4
+EXP = 384
 NSEM = 280
 
 
@@ -30,11 +30,11 @@
 
 
 def gather_chunks(s, d):
-    return (0, 1, 2, 3) if s < RZ // 2 else ((0, 1) if d == 1 else (2, 3))
+    return (0, 1) if s < RZ // 2 else ((0,) if d == 1 else (1,))
 
 
 def sum_chunks(s, d):
-    return (0, 1, 2, 3) if s > 1 else ((0, 1) if d == 1 else (2, 3))
+    return (0, 1) if s > 1 else ((0,) if d == 1 else (1,))
 
 
 def kernel(
@@ -76,10 +76,6 @@
             src_ref=dst, dst_ref=dst, send_sem=ssem.at[i], recv_sem=rsem.at[i], device_id=sibling, device_id_type=MESH
         ).wait_recv()
 
-    for a in range(2):
-        for i in range(16):
-            number(("ss", a, i))
-
     barrier = pltpu.get_barrier_semaphore()
     near = [sibling, dev(dx=1), dev(dx=-1), dev(dx=2), dev(dy=1), dev(dy=-1), dev(dy=2), dev(dz=1), dev(dz=-1)]
     for to in near:
@@ -105,9 +101,9 @@
 
     row = pl.multiple_of(g * ROWS, 64)
     for e in range(2):
-        wall[z, e * 128 : (e + 1) * 128, :] = wg_ref[e].T
-        wall[z, 256 + e * 128 : 256 + (e + 1) * 128, :] = wu_ref[e].T
-        wall[z, 512 + e * 128 : 512 + (e + 1) * 128, :] = wd_ref[e]
+        wall[z, e * EXP : e * EXP + 128, :] = wg_ref[e].T
+        wall[z, e * EXP + 128 : e * EXP + 256, :] = wu_ref[e].T
+        wall[z, e * EXP + 256 : (e + 1) * EXP, :] = wd_ref[e]
     for a, ref in enumerate((tok_ref, dout_ref)):
         for h in range(2):
             tk[a, 2 * l + h, pl.ds(row, ROWS), :] = ref[:, h * HALF : (h + 1) * HALF]
@@ -119,12 +115,16 @@
     pb[0] = jnp.zeros((8, TOK), F32)
     pl.semaphore_wait(barrier, len(near))
 
-    def wblock(b, ch):
-        return wall.at[b, pl.ds(ch * CHUNK, CHUNK), :]
-
-    for ch in range(CHUNKS):
-        for d in (1, -1):
-            put(("w", 1, d, ch), wblock(z, ch), wblock(z, ch), dev(dz=d))
+    def wblock(b, e, ch):
+        return wall.at[b, pl.ds(e * EXP + ch * CHUNK, CHUNK), :]
+
+    def start_weights(e):
+        for ch in range(2):
+            for d in (1, -1):
+                put(("w", e, 1, d, ch), wblock(z, e, ch), wblock(z, e, ch), dev(dz=d))
+
+    start_weights(0)
+    start_weights(1)
     for a in range(2):
         for d in (1, -1):
             put(("g1", a, d), block(a, (0, 0)), block(a, (0, 0)), along(a, d))
@@ -172,137 +172,94 @@
             for o2 in (0, 1, -1, 2):
                 got(("gs", a, o1, o2), block(a, rel(a, o1, o2), 1 - c))
 
-    def weights(s):
-        for ch in range(CHUNKS):
+    def weights(e, s):
+        for ch in range(2):
             for d in (1, -1):
                 if ch not in gather_chunks(s, d):
                     continue
-                where = wblock(zpos(-d * s), ch)
-                got(("w", s, d, ch), where)
+                where = wblock(zpos(-d * s), e, ch)
+                got(("w", e, s, d, ch), where)
                 if s < RZ // 2 and ch in gather_chunks(s + 1, d):
-                    put(("w", s + 1, d, ch), where, where, dev(dz=d))
-
-    def project(b1, b2, fresh=False):
+                    put(("w", e, s + 1, d, ch), where, where, dev(dz=d))
+
+    def project(e, steps, fresh=False):
+        pairs = [(z, zpos(8)) if s == 8 else (zpos(s), zpos(-s)) for s in steps]
+
         def tile(t, carry):
             rows = pl.ds(pl.multiple_of(t * 256, 256), 256)
-            for a, lo, hi in ((0, 0, 512), (1, 512, 768)):
-                lhs = jnp.concatenate([wall[b1, lo:hi, :], wall[b2, lo:hi, :]], axis=1)
-                rhs = jnp.concatenate([tk[a, b1, rows, :], tk[a, b2, rows, :]], axis=1)
-                value = nt(lhs, rhs)
-                acc[t, lo:hi, :] = value if fresh else acc[t, lo:hi, :] + value
+            for a, lo, hi in ((0, e * EXP, e * EXP + 256), (1, e * EXP + 256, (e + 1) * EXP)):
+                total = None if fresh else acc[t, lo:hi, :]
+                for b1, b2 in pairs:
+                    lhs = jnp.concatenate([wall[b1, lo:hi, :], wall[b2, lo:hi, :]], axis=1)
+                    rhs = jnp.concatenate([tk[a, b1, rows, :], tk[a, b2, rows, :]], axis=1)
+                    value = nt(lhs, rhs)
+                    total = value if total is None else total + value
+                acc[t, lo:hi, :] = total
             return carry
 
         lax.fori_loop(0, 3, tile, 0)
 
-    first(0)
-    first(1)
-    weights(1)
-    second(0, 0)
-    second(1, 0)
-    got(("wt", 0), wbr.at[0])
-    wb[1] = wb[0] + wbr[0]
-    near_x = place(x + 1 - 2 * lax.rem(x, 2), y, c, z)
-    put(("wt", 1), wb.at[1], wbr.at[1], near_x)
-    opposite(0)
-    opposite(1)
-    weights(2)
-    for o1 in (-1, 1):
-        second(0, o1)
-        second(1, o1)
-    weights(3)
-    for o1 in (0, -1):
-        across(0, o1)
-        across(1, o1)
-    second(0, 2)
-    second(1, 2)
-    weights(4)
-    for o1 in (1, 2):
-        across(0, o1)
-        across(1, o1)
-    got(("wt", 1), wbr.at[1])
-    wb[2] = wb[1] + wbr[1]
-    from_sibling(0)
-    from_sibling(1)
-    project(zpos(1), zpos(-1), True)
-    project(zpos(2), zpos(-2))
-    weights(5)
-    project(zpos(3), zpos(-3))
-    project(zpos(4), zpos(-4))
-    weights(6)
-    project(zpos(5), zpos(-5))
-    project(zpos(6), zpos(-6))
-    weights(7)
-    project(zpos(7), zpos(-7))
-    weights(8)
-    project(z, zpos(8))
-
-    for t in range(3):
-        for e in range(2):
-            f = slice(e * 128, (e + 1) * 128)
-            gate = acc[t, f, :]
-            up = acc[t, 256 + e * 128 : 256 + (e + 1) * 128, :]
-            back = acc[t, 512 + e * 128 : 512 + (e + 1) * 128, :]
+    def middle(e):
+        f = [slice(e * EXP + i * 128, e * EXP + (i + 1) * 128) for i in range(3)]
+        for t in range(3):
+            gate, up, back = (acc[t, i, :] for i in f)
             weight = wb[2, pl.ds(2 * g + e, 1), t * 256 : (t + 1) * 256]
             s = jax.nn.sigmoid(gate)
             hidden = gate * s * up
             d_hidden = weight * back
-            dct[t, f, :] = (d_hidden * up * s * (1.0 + gate * (1.0 - s))).astype(BF16)
-            dct[t, 256 + e * 128 : 256 + (e + 1) * 128, :] = (d_hidden * gate * s).astype(BF16)
-            dct[t, 512 + e * 128 : 512 + (e + 1) * 128, :] = (weight * hidden).astype(BF16)
+            dct[t, f[0], :] = (d_hidden * up * s * (1.0 + gate * (1.0 - s))).astype(BF16)
+            dct[t, f[1], :] = (d_hidden * gate * s).astype(BF16)
+            dct[t, f[2], :] = (weight * hidden).astype(BF16)
             pair = jnp.sum(hidden * back, axis=0, keepdims=True)
             pb[0, pl.ds(2 * g + e, 1), t * 256 : (t + 1) * 256] = jnp.where(weight > 0, pair, 0.0)
 
-    def products(b1, b2):
-        for a, lo, hi in ((0, 0, 512), (1, 512, 768)):
+    def products(e, b1, b2):
+        for a, lo, hi in ((0, 0, 256), (1, 256, EXP)):
             total = None
             for t in range(3):
                 rhs = jnp.concatenate(
                     [tk[a, b1, t * 256 : (t + 1) * 256, :], tk[a, b2, t * 256 : (t + 1) * 256, :]], axis=1
                 )
-                value = nn(dct[t, lo:hi, :], rhs)
+                value = nn(dct[t, e * EXP + lo : e * EXP + hi, :], rhs)
                 total = value if total is None else total + value
             term[lo:hi, :] = total
 
-    def pass_on(s):
-        products(zpos(9 - s), z if s == 1 else zpos(s - 9))
+    def pass_on(e, s):
+        products(e, zpos(9 - s), z if s == 1 else zpos(s - 9))
         if s == 1:
-            own[...] = term[:, 128:]
-        for ch in range(CHUNKS):
-            rows = slice(ch * CHUNK, (ch + 1) * CHUNK)
+            own[e * EXP : (e + 1) * EXP, :] = term[:, 128:]
+        for ch in range(2):
+            rows = slice(e * EXP + ch * CHUNK, e * EXP + (ch + 1) * CHUNK)
             for d in (1, -1):
                 k = side(d)
                 if ch not in sum_chunks(s, d):
                     continue
                 lanes = slice(0, 128) if s == 1 else slice(k * 128, (k + 1) * 128)
-                value = term[rows, lanes]
+                value = term[ch * CHUNK : (ch + 1) * CHUNK, lanes]
                 if s > 1 and ch in sum_chunks(s - 1, d):
-                    got(("r", s - 1, d, ch), zr.at[k, s - 2, rows, :])
+                    got(("r", e, s - 1, d, ch), zr.at[k, s - 2, rows, :])
                     value = value + zr[k, s - 2, rows, :].astype(F32)
                 zs[k, s - 1, rows, :] = value.astype(BF16)
-                put(("r", s, d, ch), zs.at[k, s - 1, rows, :], zr.at[k, s - 1, rows, :], dev(dz=d))
-
-    def partials(dx):
-        def one(dy, carry):
-            i = (dx % 4) * 4 + dy
-            xx, yy = lax.rem(x + dx + RX, RX), lax.rem(y + dy, RY)
-            ll = lax.div(xx, 2) * 4 + yy
-            base = lax.rem(xx, 2) * 2
-            mine = pl.multiple_of((base + c) * ROWS, 64)
-            theirs = pl.multiple_of((base + 1 - c) * ROWS, 64)
-            lhs = jnp.concatenate([am[pl.ds(mine, ROWS), :], am[pl.ds(theirs, ROWS), :]], axis=0)
-            for a, lo, hi in ((0, 512, 768), (1, 0, 512)):
-                rhs = jnp.concatenate([wall[2 * ll, lo:hi, :], wall[2 * ll + 1, lo:hi, :]], axis=1)
-                value = nn(lhs[:, lo:hi], rhs)
-                op[a, i] = value[:ROWS]
-                ss[a, i] = value[ROWS:].astype(BF16)
-                k = a * 16 + i
-                pltpu.make_async_remote_copy(
-                    src_ref=ss.at[a, i], dst_ref=sr.at[a, i], send_sem=ssem.at[k], recv_sem=rsem.at[k],
-                    device_id=sibling, device_id_type=MESH,
-                ).start()
-            return carry
-
-        lax.fori_loop(0, 4, one, 0)
+                put(("r", e, s, d, ch), zs.at[k, s - 1, rows, :], zr.at[k, s - 1, rows, :], dev(dz=d))
+
+    def partial(a, o1, o2):
+        i = (o1 % 4) * 4 + o2 if a == 0 else o2 * 4 + o1 % 4
+        dx, dy = (o1, o2) if a == 0 else (o2, o1)
+        xx, yy = lax.rem(x + dx + RX, RX), lax.rem(y + dy + RY, RY)
+        ll = lax.div(xx, 2) * 4 + yy
+        base = lax.rem(xx, 2) * 2
+        mine = pl.ds(pl.multiple_of((base + c) * ROWS, 64), ROWS)
+        theirs = pl.ds(pl.multiple_of((base + 1 - c) * ROWS, 64), ROWS)
+        lo, hi = (256, EXP) if a == 0 else (0, 256)
+        cols = [slice(e * EXP + lo, e * EXP + hi) for e in range(2)]
+        lhs = jnp.concatenate([jnp.concatenate([am[r, k] for k in cols], axis=1) for r in (mine, theirs)], axis=0)
+        rhs = jnp.concatenate(
+            [jnp.concatenate([wall[2 * ll + h, k, :] for k in cols], axis=0) for h in range(2)], axis=1
+        )
+        value = nn(lhs, rhs)
+        op[a, i] = value[:ROWS]
+        ss[a, i] = value[ROWS:].astype(BF16)
+        put(("ss", a, i), ss.at[a, i], sr.at[a, i], sibling)
 
     def whole(a, o1, o2):
         ox, oy = rel(a, o1, o2)
@@ -358,6 +315,7 @@
             value = value + r2f[a, side(d)].astype(F32)
         ref[...] = value.astype(BF16)
 
+    near_x = place(x + 1 - 2 * lax.rem(x, 2), y, c, z)
     partner = [
         sibling, near_x, dev(dx=2), place(x, y + 1 - 2 * lax.rem(y, 2), c, z), dev(dy=2),
     ]
@@ -375,59 +333,118 @@
             for j in range(2):
                 pair_ref[j : j + 1, :] = jnp.sum(jnp.where(picked[j], mine, 0.0), axis=0, keepdims=True)
 
-    pass_on(1)
-    share(0)
-    for t in range(3):
+    def each(what, *orders):
+        for o in orders:
+            for a in range(2):
+                what(a, o)
+
+    def partials(a, o1):
+        for o2 in (2, 1, 3, 0):
+            partial(a, o1, o2)
+
+    def turned(t):
         for u in range(6):
             am[t * 256 : (t + 1) * 256, u * 128 : (u + 1) * 128] = dct[t, u * 128 : (u + 1) * 128, :].T
-    pass_on(2)
-    partials(2)
+
+    first(0)
+    first(1)
+    weights(0, 1)
+    each(second, 0)
+    got(("wt", 0), wbr.at[0])
+    wb[1] = wb[0] + wbr[0]
+    put(("wt", 1), wb.at[1], wbr.at[1], near_x)
+    weights(1, 1)
+    opposite(0)
+    opposite(1)
+    weights(0, 2)
+    each(second, -1)
+    weights(1, 2)
+    each(second, 1)
+    weights(0, 3)
+    each(across, 0)
+    weights(1, 3)
+    each(second, 2)
+    each(across, -1)
+    weights(0, 4)
+    each(across, 1)
+    weights(1, 4)
+    each(across, 2)
+    weights(0, 5)
+    got(("wt", 1), wbr.at[1])
+    wb[2] = wb[1] + wbr[1]
+    from_sibling(0)
+    from_sibling(1)
+    weights(1, 5)
+    project(0, (1, 2, 3), True)
+    weights(0, 6)
+    project(1, (1, 2, 3), True)
+    weights(1, 6)
+    project(0, (4, 5, 6))
+    weights(0, 7)
+    project(1, (4, 5, 6))
+    weights(1, 7)
+    project(0, (7,))
+    weights(0, 8)
+    project(0, (8,))
+    middle(0)
+    pass_on(0, 1)
+    weights(1, 8)
+    project(1, (7, 8))
+    middle(1)
+    pass_on(1, 1)
+    share(0)
+    turned(0)
+    turned(1)
+    turned(2)
+    pass_on(0, 2)
+    each(partials, 2)
+    pass_on(1, 2)
+    each(far, 2, 1)
+    partials(0, 1)
+    pass_on(0, 3)
+    each(far, 3, 0)
+    partials(1, 1)
+    pass_on(1, 3)
     share(1)
-    pass_on(3)
-    partials(1)
-    partials(-1)
+    partials(0, -1)
+    pass_on(0, 4)
+    partials(1, -1)
+    pass_on(1, 4)
+    each(next_to, 2, 1)
+    pass_on(0, 5)
+    each(next_to, 3, 0)
     share(2)
-    partials(0)
-    pass_on(4)
-    for o2 in (2, 1, 3, 0):
-        for a in range(2):
-            far(a, o2)
+    pass_on(1, 5)
+    partials(0, 0)
+    pass_on(0, 6)
+    partials(1, 0)
+    each(here, 2)
+    pass_on(1, 6)
+    each(here, 1, 3)
     share(3)
-    pass_on(5)
-    for o2 in (2, 1, 3, 0):
-        for a in range(2):
-            next_to(a, o2)
+    pass_on(0, 7)
+    each(here, 0)
+    pass_on(1, 7)
+    turn(0)
+    turn(1)
     share(4)
-    pass_on(6)
-    for o2 in (2, 1, 3):
-        for a in range(2):
-            here(a, o2)
+    pass_on(0, 8)
     share(5)
-    pass_on(7)
-    for a in range(2):
-        here(a, 0)
-        turn(a)
-    pass_on(8)
+    pass_on(1, 8)
     finish(0, moe_ref)
     finish(1, gtok_ref)
-    for ch in range(CHUNKS):
-        for d in (1, -1):
-            got(("r", 8, d, ch), zr.at[side(d), 7, pl.ds(ch * CHUNK, CHUNK), :])
     for e in range(2):
-        for base, ref in ((0, gg_ref), (256, gu_ref), (512, gd_ref)):
-            rows = slice(base + e * 128, base + (e + 1) * 128)
+        for ch in range(2):
+            for d in (1, -1):
+                got(("r", e, 8, d, ch), zr.at[side(d), 7, pl.ds(e * EXP + ch * CHUNK, CHUNK), :])
+    for e in range(2):
+        for base, ref in ((0, gg_ref), (128, gu_ref), (256, gd_ref)):
+            rows = slice(e * EXP + base, e * EXP + base + 128)
             value = own[rows, :] + zr[0, 7, rows, :].astype(F32) + zr[1, 7, rows, :].astype(F32)
-            ref[e] = value if base == 512 else value.T
+            ref[e] = value if base == 256 else value.T
 
     for made in sent:
         made.wait_send()
-    for a in range(2):
-        for i in range(16):
-            k = a * 16 + i
-            pltpu.make_async_remote_copy(
-                src_ref=ss.at[a, i], dst_ref=sr.at[a, i], send_sem=ssem.at[k], recv_sem=rsem.at[k],
-                device_id=sibling, device_id_type=MESH,
-            ).wait_send()
     assert len(numbers) <= NSEM, len(numbers)
 
 
@@ -457,7 +474,7 @@
             pltpu.VMEM((3, HID, 256), F32),
             pltpu.VMEM((3, HID, 256), BF16),
             pltpu.VMEM((TOK, HID), BF16),
-            pltpu.VMEM((HID, 256), F32),
+            pltpu.VMEM((EXP, 256), F32),
             pltpu.VMEM((HID, 128), F32),
             pltpu.VMEM((2, 8, HID, 128), BF16),
             pltpu.VMEM((2, 8, HID, 128), BF16),

time: 110 us -> 100 us (0.909)
  Pallas kernels: 109 us -> 99 us
    pallas_call x1, Pallas kernels: 107 us -> 97 us  [body(): pl.pallas_call(kernel, out_shape=(shape(tokens.shape, BF16), shape(tokens...]
where the time goes in v4:
time: 100 us; the launch traced here: 99.6 us
  Pallas kernels  99 us (99%)
    pallas_call x1, Pallas kernels, body(): pl.pallas_call(kernel, out_shape=(shape(tokens.shape, BF16), shape(tokens...  97 us

profile of v4, /device:TPU:6, one launch (start us, length us, event | category | flops | bytes accessed | tf_op | source)
XLA Modules:
  0.0 99.6 jit_solution(17601587453556656015)
XLA Ops:
  0.6 97.0 %shard_map.118 = (bf16[192,256]{1,0:T(8,128)(2,1)}, bf16[192,256]{1,0:T(8,128)(2,1)}, f32[2,128,128]{2,1,0:T(8,128)}, f32[2,128,128]{2,1,0:T(8,128)}, f32[2,128,128]{2,1,0:T(8,128)}, /*index=5*/f32[2,192]{1,0:T(2,128)}) custom-call(bf16[192,256]{1,0:T(8,128)(2,1)} %tok_ref.1, bf16[192,256]{1,0:T(8,128)(2,1)} %dout_ref.1, bf16[2,128,128]{2,1,0:T(8,128)(2,1)} %wg_ref.1, ...), custom_call_target="tpu_custom_call" | custom-call | tf_op jit(solution)/shard_map/pallas_call | solution.py:459
  97.7 1.9 %shard_map.119 = (bf16[192,256]{1,0:T(8,128)(2,1)}, bf16[192,256]{1,0:T(8,128)(2,1)}, f32[2,128,128]{2,1,0:T(8,128)}, f32[2,128,128]{2,1,0:T(8,128)}, f32[2,128,128]{2,1,0:T(8,128)}, /*index=5*/f32[2,192]{1,0:T(2,128)}) custom-call(bf16[192,256]{1,0:T(8,128)(2,1)} %get-tuple-element.18.refs_0_, bf16[192,256]{1,0:T(8,128)(2,1)} %get-tuple-element.19.refs_1_, ...), custom_call_target="tpu_custom_call" | custom-call | tf_op jit(solution)/shard_map/pallas_call | solution.py:505

commit v5 on v4

--- a/solution.py
+++ b/solution.py
@@ -41,7 +41,8 @@
     tok_ref, dout_ref, wg_ref, wu_ref, wd_ref, ids_ref, gates_ref,
     moe_ref, gtok_ref, gg_ref, gu_ref, gd_ref, pair_ref,
     tk, wall, acc, dct, am, term, own, zs, zr, ss, sr, op, s1h, r1h, s1f, r1f, op2,
-    s2h, r2h, s2f, r2f, wb, wbr, pb, pbr, ssem, rsem,
+    s2h, r2h, s2f, r2f, wb, wbr, pb, pbr, wtmp, ids_in, gates_in, rows_out, grads_out, pair_out,
+    ssem, rsem, isem, osem,
 ):
     g, z, l = lax.axis_index("group"), lax.axis_index("blk"), lax.axis_index("local")
     x = lax.div(l, 4) * 2 + lax.div(g, 2)
@@ -76,6 +77,10 @@
             src_ref=dst, dst_ref=dst, send_sem=ssem.at[i], recv_sem=rsem.at[i], device_id=sibling, device_id_type=MESH
         ).wait_recv()
 
+    for a in range(2):
+        for i in range(16):
+            number(("ss", a, i))
+
     barrier = pltpu.get_barrier_semaphore()
     near = [sibling, dev(dx=1), dev(dx=-1), dev(dx=2), dev(dy=1), dev(dy=-1), dev(dy=2), dev(dz=1), dev(dz=-1)]
     for to in near:
@@ -100,16 +105,35 @@
         return tk.at[a, 2 * ll + h, pl.ds(row, ROWS), :]
 
     row = pl.multiple_of(g * ROWS, 64)
+    fetched, leaving = [], []
+
+    def leave(src, dst):
+        made = pltpu.make_async_copy(src, dst, osem.at[len(leaving)])
+        made.start()
+        leaving.append(made)
+
+    def fetch(src, dst):
+        made = pltpu.make_async_copy(src, dst, isem.at[len(fetched)])
+        made.start()
+        fetched.append(made)
+
+    fetch(wg_ref, wtmp.at[0])
+    fetch(wu_ref, wtmp.at[1])
     for e in range(2):
-        wall[z, e * EXP : e * EXP + 128, :] = wg_ref[e].T
-        wall[z, e * EXP + 128 : e * EXP + 256, :] = wu_ref[e].T
-        wall[z, e * EXP + 256 : (e + 1) * EXP, :] = wd_ref[e]
+        fetch(wd_ref.at[e], wall.at[z, pl.ds(e * EXP + 256, 128), :])
+    fetch(ids_ref, ids_in)
+    fetch(gates_ref, gates_in)
     for a, ref in enumerate((tok_ref, dout_ref)):
         for h in range(2):
-            tk[a, 2 * l + h, pl.ds(row, ROWS), :] = ref[:, h * HALF : (h + 1) * HALF]
+            fetch(ref.at[:, pl.ds(h * HALF, HALF)], tk.at[a, 2 * l + h, pl.ds(row, ROWS), :])
+    for made in fetched:
+        made.wait()
+    for e in range(2):
+        wall[z, e * EXP : e * EXP + 128, :] = wtmp[0, e].T
+        wall[z, e * EXP + 128 : e * EXP + 256, :] = wtmp[1, e].T
     number_of = lax.broadcasted_iota(jnp.int32, (8, ROWS), 0)
-    picked = [ids_ref[k : k + 1, :] == number_of for k in range(2)]
-    weights_of = jnp.where(picked[0], gates_ref[0:1, :], 0.0) + jnp.where(picked[1], gates_ref[1:2, :], 0.0)
+    picked = [ids_in[k : k + 1, :] == number_of for k in range(2)]
+    weights_of = jnp.where(picked[0], gates_in[0:1, :], 0.0) + jnp.where(picked[1], gates_in[1:2, :], 0.0)
     for q in range(4):
         wb[0, :, q * ROWS : (q + 1) * ROWS] = jnp.where(g == q, weights_of, 0.0)
     pb[0] = jnp.zeros((8, TOK), F32)
@@ -222,25 +246,42 @@
                 )
                 value = nn(dct[t, e * EXP + lo : e * EXP + hi, :], rhs)
                 total = value if total is None else total + value
-            term[lo:hi, :] = total
-
-    def pass_on(e, s):
+            term[e, lo:hi, :] = total
+
+    def begin(e, s):
         products(e, zpos(9 - s), z if s == 1 else zpos(s - 9))
         if s == 1:
-            own[e * EXP : (e + 1) * EXP, :] = term[:, 128:]
+            own[e * EXP : (e + 1) * EXP, :] = term[e, :, 128:]
+        for d in (1, -1):
+            for ch in sum_chunks(s, d):
+                if s == 1 or ch not in sum_chunks(s - 1, d):
+                    step(e, s, d, ch, False)
+
+    def step(e, s, d, ch, more):
+        k = side(d)
+        rows = slice(e * EXP + ch * CHUNK, e * EXP + (ch + 1) * CHUNK)
+        lanes = slice(0, 128) if s == 1 else slice(k * 128, (k + 1) * 128)
+        value = term[e, ch * CHUNK : (ch + 1) * CHUNK, lanes]
+        if more:
+            got(("r", e, s - 1, d, ch), zr.at[k, s - 2, rows, :])
+            value = value + zr[k, s - 2, rows, :].astype(F32)
+        zs[k, s - 1, rows, :] = value.astype(BF16)
+        put(("r", e, s, d, ch), zs.at[k, s - 1, rows, :], zr.at[k, s - 1, rows, :], dev(dz=d))
+
+    def pass_on(e, s):
+        if s > 2:
+            begin(e, s)
         for ch in range(2):
-            rows = slice(e * EXP + ch * CHUNK, e * EXP + (ch + 1) * CHUNK)
             for d in (1, -1):
-                k = side(d)
-                if ch not in sum_chunks(s, d):
-                    continue
-                lanes = slice(0, 128) if s == 1 else slice(k * 128, (k + 1) * 128)
-                value = term[ch * CHUNK : (ch + 1) * CHUNK, lanes]
-                if s > 1 and ch in sum_chunks(s - 1, d):
-                    got(("r", e, s - 1, d, ch), zr.at[k, s - 2, rows, :])
-                    value = value + zr[k, s - 2, rows, :].astype(F32)
-                zs[k, s - 1, rows, :] = value.astype(BF16)
-                put(("r", e, s, d, ch), zs.at[k, s - 1, rows, :], zr.at[k, s - 1, rows, :], dev(dz=d))
+                if ch in sum_chunks(s - 1, d):
+                    step(e, s, d, ch, True)
+
+    def handed(a, i):
+        k = a * 16 + i
+        return pltpu.make_async_remote_copy(
+            src_ref=ss.at[a, i], dst_ref=sr.at[a, i], send_sem=ssem.at[k], recv_sem=rsem.at[k],
+            device_id=sibling, device_id_type=MESH,
+        )
 
     def partial(a, o1, o2):
         i = (o1 % 4) * 4 + o2 if a == 0 else o2 * 4 + o1 % 4
@@ -259,7 +300,7 @@
         value = nn(lhs, rhs)
         op[a, i] = value[:ROWS]
         ss[a, i] = value[ROWS:].astype(BF16)
-        put(("ss", a, i), ss.at[a, i], sr.at[a, i], sibling)
+        handed(a, i).start()
 
     def whole(a, o1, o2):
         ox, oy = rel(a, o1, o2)
@@ -313,7 +354,8 @@
         for d in (1, -1):
             got(("p2f", a, d), r2f.at[a, side(d)])
             value = value + r2f[a, side(d)].astype(F32)
-        ref[...] = value.astype(BF16)
+        rows_out[a] = value.astype(BF16)
+        leave(rows_out.at[a], ref)
 
     near_x = place(x + 1 - 2 * lax.rem(x, 2), y, c, z)
     partner = [
@@ -331,7 +373,8 @@
             for q in range(4):
                 mine = jnp.where(g == q, pb[k, :, q * ROWS : (q + 1) * ROWS], mine)
             for j in range(2):
-                pair_ref[j : j + 1, :] = jnp.sum(jnp.where(picked[j], mine, 0.0), axis=0, keepdims=True)
+                pair_out[j : j + 1, :] = jnp.sum(jnp.where(picked[j], mine, 0.0), axis=0, keepdims=True)
+            leave(pair_out, pair_ref)
 
     def each(what, *orders):
         for o in orders:
@@ -339,8 +382,11 @@
                 what(a, o)
 
     def partials(a, o1):
-        for o2 in (2, 1, 3, 0):
-            partial(a, o1, o2)
+        def one(k, carry):
+            partial(a, o1, lax.rem(k + 2, 4))
+            return carry
+
+        lax.fori_loop(0, 4, one, 0)
 
     def turned(t):
         for u in range(6):
@@ -387,74 +433,92 @@
     weights(0, 8)
     project(0, (8,))
     middle(0)
-    pass_on(0, 1)
+    begin(0, 1)
+    begin(0, 2)
     weights(1, 8)
     project(1, (7, 8))
     middle(1)
-    pass_on(1, 1)
+    begin(1, 1)
+    begin(1, 2)
     share(0)
     turned(0)
     turned(1)
     turned(2)
+    partials(0, 2)
     pass_on(0, 2)
-    each(partials, 2)
+    partials(1, 2)
+    each(far, 2)
     pass_on(1, 2)
-    each(far, 2, 1)
+    each(far, 1, 3)
     partials(0, 1)
     pass_on(0, 3)
-    each(far, 3, 0)
+    each(far, 0)
     partials(1, 1)
+    share(1)
     pass_on(1, 3)
-    share(1)
     partials(0, -1)
     pass_on(0, 4)
     partials(1, -1)
+    each(next_to, 2)
     pass_on(1, 4)
-    each(next_to, 2, 1)
+    each(next_to, 1, 3)
+    share(2)
     pass_on(0, 5)
-    each(next_to, 3, 0)
-    share(2)
+    each(next_to, 0)
+    partials(0, 0)
     pass_on(1, 5)
-    partials(0, 0)
-    pass_on(0, 6)
     partials(1, 0)
     each(here, 2)
-    pass_on(1, 6)
+    pass_on(0, 6)
     each(here, 1, 3)
     share(3)
+    pass_on(1, 6)
+    each(here, 0)
     pass_on(0, 7)
-    each(here, 0)
-    pass_on(1, 7)
     turn(0)
     turn(1)
     share(4)
+    pass_on(1, 7)
+    share(5)
     pass_on(0, 8)
-    share(5)
-    pass_on(1, 8)
     finish(0, moe_ref)
     finish(1, gtok_ref)
+    pass_on(1, 8)
     for e in range(2):
         for ch in range(2):
             for d in (1, -1):
                 got(("r", e, 8, d, ch), zr.at[side(d), 7, pl.ds(e * EXP + ch * CHUNK, CHUNK), :])
-    for e in range(2):
         for base, ref in ((0, gg_ref), (128, gu_ref), (256, gd_ref)):
             rows = slice(e * EXP + base, e * EXP + base + 128)
             value = own[rows, :] + zr[0, 7, rows, :].astype(F32) + zr[1, 7, rows, :].astype(F32)
-            ref[e] = value if base == 256 else value.T
-
+            grads_out[base // 128, e] = value if base == 256 else value.T
+            leave(grads_out.at[base // 128, e], ref.at[e])
+
+    for made in leaving:
+        made.wait()
     for made in sent:
         made.wait_send()
+    for a in range(2):
+        for i in range(16):
+            handed(a, i).wait_send()
     assert len(numbers) <= NSEM, len(numbers)
 
 
 def hand_over(*refs):
-    for src, dst in zip(refs[:6], refs[6:]):
-        dst[...] = src[...]
+    src, dst, held, sem = refs[:6], refs[6:12], refs[12:18], refs[18]
+    into = [pltpu.make_async_copy(src[i], held[i], sem.at[i]) for i in range(6)]
+    out = [pltpu.make_async_copy(held[i], dst[i], sem.at[6 + i]) for i in range(6)]
+    for one in into:
+        one.start()
+    for i in range(6):
+        into[i].wait()
+        out[i].start()
+    for one in out:
+        one.wait()
 
 
 def body(tokens, d_out, ids, gates, w_gate, w_up, w_down):
-    vm = pl.BlockSpec(memory_space=pltpu.VMEM)
+    anywhere = pl.BlockSpec(memory_space=pl.ANY)
     shape = jax.ShapeDtypeStruct
     moe, gtok, gg, gu, gd, pair = pl.pallas_call(
         kernel,
@@ -466,15 +530,15 @@
             shape(w_down.shape, F32),
             shape(gates.shape[::-1], F32),
         ),
-        in_specs=[vm] * 7,
-        out_specs=(vm,) * 6,
+        in_specs=[anywhere] * 7,
+        out_specs=(anywhere,) * 6,
         scratch_shapes=[
             pltpu.VMEM((2, 16, TOK, 128), BF16),
             pltpu.VMEM((16, HID, 128), BF16),
             pltpu.VMEM((3, HID, 256), F32),
             pltpu.VMEM((3, HID, 256), BF16),
             pltpu.VMEM((TOK, HID), BF16),
-            pltpu.VMEM((EXP, 256), F32),
+            pltpu.VMEM((2, EXP, 256), F32),
             pltpu.VMEM((HID, 128), F32),
             pltpu.VMEM((2, 8, HID, 128), BF16),
             pltpu.VMEM((2, 8, HID, 128), BF16),
@@ -494,8 +558,16 @@
             pltpu.VMEM((2, 8, TOK), F32),
             pltpu.VMEM((6, 8, TOK), F32),
             pltpu.VMEM((5, 8, TOK), F32),
+            pltpu.VMEM((2, 2, 128, 128), BF16),
+            pltpu.VMEM((2, ROWS), jnp.int32),
+            pltpu.VMEM((2, ROWS), F32),
+            pltpu.VMEM((2, ROWS, COLS), BF16),
+            pltpu.VMEM((3, 2, 128, 128), F32),
+            pltpu.VMEM((2, ROWS), F32),
             pltpu.SemaphoreType.DMA((NSEM,)),
             pltpu.SemaphoreType.DMA((NSEM,)),
+            pltpu.SemaphoreType.DMA((12,)),
+            pltpu.SemaphoreType.DMA((9,)),
         ],
         compiler_params=pltpu.CompilerParams(
             collective_id=0, has_side_effects=True, vmem_limit_bytes=58 * 2**20
@@ -505,8 +577,9 @@
     moe, gtok, gg, gu, gd, pair = pl.pallas_call(
         hand_over,
         out_shape=tuple(shape(a.shape, a.dtype) for a in made),
-        in_specs=[vm] * 6,
-        out_specs=(vm,) * 6,
+        in_specs=[anywhere] * 6,
+        out_specs=(anywhere,) * 6,
+        scratch_shapes=[pltpu.VMEM(a.shape, a.dtype) for a in made] + [pltpu.SemaphoreType.DMA((12,))],
         compiler_params=pltpu.CompilerParams(vmem_limit_bytes=58 * 2**20),
     )(*made)
     return (moe, gtok, pair.T, gg, gu, gd)

time: 100 us -> 98.4 us (0.984); the launches traced: 99.6 us -> 96.9 us
  Pallas kernels: 99 us -> 96.3 us
    pallas_call x1, Pallas kernels: 97 us -> 94.4 us  [body(): pl.pallas_call(kernel, out_shape=(shape(tokens.shape, BF16), shape(tokens...]
where the time goes in v5:
time: 98.4 us; the launch traced here: 96.9 us
  Pallas kernels  96.3 us (98%)
    pallas_call x1, Pallas kernels, body(): pl.pallas_call(kernel, out_shape=(shape(tokens.shape, BF16), shape(tokens...  94.4 us

profile of v5, /device:TPU:6, one launch (start us, length us, event | category | flops | bytes accessed | tf_op | source)
XLA Modules:
  0.0 96.9 jit_solution(7164121034267796383)
XLA Ops:
  0.6 94.4 %shard_map.118 = (bf16[192,256]{1,0:T(8,128)(2,1)}, bf16[192,256]{1,0:T(8,128)(2,1)}, f32[2,128,128]{2,1,0:T(8,128)}, f32[2,128,128]{2,1,0:T(8,128)}, f32[2,128,128]{2,1,0:T(8,128)}, /*index=5*/f32[2,192]{1,0:T(2,128)}) custom-call(bf16[192,256]{1,0:T(8,128)(2,1)} %tok_ref.1, bf16[192,256]{1,0:T(8,128)(2,1)} %dout_ref.1, bf16[2,128,128]{2,1,0:T(8,128)(2,1)} %wg_ref.1, ...), custom_call_target="tpu_custom_call" | custom-call | tf_op jit(solution)/shard_map/pallas_call | solution.py:523
  95.0 1.9 %shard_map.119 = (bf16[192,256]{1,0:T(8,128)(2,1)}, bf16[192,256]{1,0:T(8,128)(2,1)}, f32[2,128,128]{2,1,0:T(8,128)}, f32[2,128,128]{2,1,0:T(8,128)}, f32[2,128,128]{2,1,0:T(8,128)}, /*index=5*/f32[2,192]{1,0:T(2,128)}) custom-call(bf16[192,256]{1,0:T(8,128)(2,1)} %get-tuple-element.18.refs_0_, bf16[192,256]{1,0:T(8,128)(2,1)} %get-tuple-element.19.refs_1_, ...), custom_call_target="tpu_custom_call" | custom-call | tf_op jit(solution)/shard_map/pallas_call | solution.py:577

commit v6 on v5

--- a/solution.py
+++ b/solution.py
@@ -269,12 +269,12 @@
         put(("r", e, s, d, ch), zs.at[k, s - 1, rows, :], zr.at[k, s - 1, rows, :], dev(dz=d))
 
     def pass_on(e, s):
-        if s > 2:
-            begin(e, s)
         for ch in range(2):
             for d in (1, -1):
                 if ch in sum_chunks(s - 1, d):
                     step(e, s, d, ch, True)
+        if s < RZ // 2:
+            products(e, zpos(8 - s), zpos(s - 8))
 
     def handed(a, i):
         k = a * 16 + i

time: 98.4 us -> 98.4 us (level)
  no operation moved by 1% of the time
where the time goes in v6:
time: 98.4 us; the launch traced here: 96.7 us
  Pallas kernels  96 us (98%)
    pallas_call x1, Pallas kernels, body(): pl.pallas_call(kernel, out_shape=(shape(tokens.shape, BF16), shape(tokens...  94.1 us

profile of v6, /device:TPU:6, one launch (start us, length us, event | category | flops | bytes accessed | tf_op | source)
XLA Modules:
  0.0 96.7 jit_solution(14589914795358778074)
XLA Ops:
  0.6 94.1 %shard_map.118 = (bf16[192,256]{1,0:T(8,128)(2,1)}, bf16[192,256]{1,0:T(8,128)(2,1)}, f32[2,128,128]{2,1,0:T(8,128)}, f32[2,128,128]{2,1,0:T(8,128)}, f32[2,128,128]{2,1,0:T(8,128)}, /*index=5*/f32[2,192]{1,0:T(2,128)}) custom-call(bf16[192,256]{1,0:T(8,128)(2,1)} %tok_ref.1, bf16[192,256]{1,0:T(8,128)(2,1)} %dout_ref.1, bf16[2,128,128]{2,1,0:T(8,128)(2,1)} %wg_ref.1, ...), custom_call_target="tpu_custom_call" | custom-call | tf_op jit(solution)/shard_map/pallas_call | solution.py:523
  94.8 1.9 %shard_map.119 = (bf16[192,256]{1,0:T(8,128)(2,1)}, bf16[192,256]{1,0:T(8,128)(2,1)}, f32[2,128,128]{2,1,0:T(8,128)}, f32[2,128,128]{2,1,0:T(8,128)}, f32[2,128,128]{2,1,0:T(8,128)}, /*index=5*/f32[2,192]{1,0:T(2,128)}) custom-call(bf16[192,256]{1,0:T(8,128)(2,1)} %get-tuple-element.18.refs_0_, bf16[192,256]{1,0:T(8,128)(2,1)} %get-tuple-element.19.refs_1_, ...), custom_call_target="tpu_custom_call" | custom-call | tf_op jit(solution)/shard_map/pallas_call | solution.py:577
